TPU v7x, 256 devices: a whole 4x4x8 slice. The times are simulated.
256 devices in a mesh: fsdp: 8 (over y, x_lo), ctx: 32 (over z, x_hi, core).
Axes of the slice: x: 4 (x_hi: 2, x_lo: 2; x = x_hi * 2 + x_lo), y: 4, z: 8, core: 2. Of those that a mesh axis runs over, the one named last changes fastest.
Arguments:
- tokens: bfloat16 [8, 8192, 2048], P('fsdp', 'ctx'), may hold values from -6 to 6
- zx_weight: bfloat16 [2048, 4096], P(None, ('fsdp', 'ctx')), may hold values from -0.125 to 0.125
- bc_weight: bfloat16 [2048, 512], P(None, ('fsdp', 'ctx')), may hold values from -0.01171875 to 0.01171875
- dt_weight: bfloat16 [2048, 64], replicated, may hold values from -0.125 to 0.125
- decay_rate: float32 [32], replicated, may hold values from 2.3193359e-05 to 0.067
- skip_gain: float32 [32], replicated, may hold values from 0.5 to 2
- norm_gain: float32 [2048], replicated, may hold values from 0.25 to 1.75
- out_weight: bfloat16 [2048, 2048], P(None, ('fsdp', 'ctx')), may hold values from -0.125 to 0.125
Outputs:
- mixed: bfloat16 [8, 8192, 2048], P('fsdp', 'ctx')
All inputs are finite; a program needn't handle non-finite values.
Results may differ from a plain program's by a relative error of at most 0.0087.
Values may be sent and summed in bfloat16 or wider, within the bound.
A program may use at most 256 MiB of HBM per device.

v0:
```python
import jax
import jax.numpy as jnp
from jax import lax
from jax.sharding import PartitionSpec as P

BLOCK = 128


def entering_2(value, axis, join, neutral, backward):
    count, mine = (lax.axis_size(axis), lax.axis_index(axis))
    pieces = jax.tree.map(lambda part: lax.all_gather(part, axis), value)
    if backward:
        pieces = jax.tree.map(lambda part: part[::-1], pieces)
        mine = count - 1 - mine
    total = jax.tree.map(
        lambda part, zero: jnp.full_like(part, 0) + jnp.asarray(zero, part.dtype), value, neutral
    )

    def hop(position, total):
        longer = join(total, jax.tree.map(lambda part: part[position], pieces))
        return jax.tree.map(lambda new, old: jnp.where(position < mine, new, old), longer, total)

    return lax.fori_loop(0, count - 1, hop, total)


def prepare(inner, b_rows, c_rows, step_size, decay_rate):
    length = inner.shape[0]
    heads = decay_rate.shape[0]
    head_size = inner.shape[1] // heads
    state_size = b_rows.shape[1]
    block_count = length // BLOCK
    inner_blocks = inner.reshape(block_count, BLOCK, heads, head_size)
    b_blocks = b_rows.reshape(block_count, BLOCK, state_size)
    c_blocks = c_rows.reshape(block_count, BLOCK, state_size)
    step_blocks = step_size.reshape(block_count, BLOCK, heads)
    log_decay = jnp.cumsum(-step_blocks * decay_rate[None, None, :], axis=1)
    log_heads = jnp.swapaxes(log_decay, 1, 2)
    step_heads = jnp.swapaxes(step_blocks, 1, 2)
    log_end = log_decay[:, -1, :]
    positions = jnp.arange(BLOCK)
    strict_mask = positions[:, None] > positions[None, :]
    intersection = jnp.einsum(
        "ctn,csn->cts", c_blocks, b_blocks, preferred_element_type=jnp.float32
    )
    log_gap = log_heads[:, :, :, None] - log_heads[:, :, None, :]
    decayed = jnp.exp(jnp.where(strict_mask[None, None], log_gap, -jnp.inf))
    weights = (intersection[:, None] * decayed * step_heads[:, :, None, :]).astype(jnp.bfloat16)
    y_intra = jnp.einsum(
        "chts,cshp->cthp", weights, inner_blocks, preferred_element_type=jnp.float32
    )
    factor = jnp.exp(log_end[:, None, :] - log_decay) * step_blocks
    scaled_inner = (factor[..., None] * inner_blocks).astype(jnp.bfloat16)
    k_state = jnp.einsum(
        "cshp,csn->chpn", scaled_inner, b_blocks, preferred_element_type=jnp.float32
    )
    block_decay = jnp.exp(log_end)
    total_decay = jnp.ones((heads,), jnp.float32)
    summary = jnp.zeros((heads, head_size, state_size), jnp.float32)
    for block_id in range(block_count):
        summary = block_decay[block_id][:, None, None] * summary + k_state[block_id]
        total_decay = total_decay * block_decay[block_id]
    return ((log_decay, c_blocks, y_intra, k_state, block_decay), (total_decay, summary))


def finish(pieces, state_in):
    log_decay, c_blocks, y_intra, k_state, block_decay = pieces
    block_count = k_state.shape[0]
    entering = []
    state = state_in
    for block_id in range(block_count):
        entering.append(state)
        state = block_decay[block_id][:, None, None] * state + k_state[block_id]
    states_low = jnp.stack(entering).astype(jnp.bfloat16)
    y_inter = jnp.exp(log_decay)[..., None] * jnp.einsum(
        "ctn,chpn->cthp", c_blocks, states_low, preferred_element_type=jnp.float32
    )
    summed = y_intra + y_inter
    return summed.reshape(summed.shape[0] * summed.shape[1], summed.shape[2] * summed.shape[3])


def chain(earlier, later):
    return (earlier[0] * later[0], later[0][:, None, None] * earlier[1] + later[1])


def shards(tokens, zx_weight, bc_weight, dt_weight, decay_rate, skip_gain, norm_gain, out_weight):
    token_rows = tokens[0]

    def project(piece):
        return jnp.dot(token_rows, piece, preferred_element_type=jnp.float32).astype(jnp.bfloat16)

    zx_proj = project(lax.all_gather(zx_weight, ("fsdp", "ctx"), axis=1, tiled=True))
    bc_proj = project(lax.all_gather(bc_weight, ("fsdp", "ctx"), axis=1, tiled=True))
    dt_raw = jnp.dot(token_rows, dt_weight, preferred_element_type=jnp.float32).astype(jnp.bfloat16)
    width = zx_proj.shape[1] // 2
    heads = decay_rate.shape[0]
    head_size = width // heads
    state_size = bc_proj.shape[1] // 4
    gate = zx_proj[:, :width]
    inner = zx_proj[:, width:]
    dt_fwd = jax.nn.softplus(dt_raw[:, :heads].astype(jnp.float32))
    dt_bwd = jax.nn.softplus(dt_raw[:, heads:].astype(jnp.float32))
    fwd_b = bc_proj[:, :state_size]
    fwd_c = bc_proj[:, state_size : 2 * state_size]
    bwd_b = bc_proj[:, 2 * state_size : 3 * state_size]
    bwd_c = bc_proj[:, 3 * state_size :]
    fwd_parts, fwd_summary = prepare(inner, fwd_b, fwd_c, dt_fwd, decay_rate)
    bwd_parts, bwd_summary = prepare(
        inner[::-1], bwd_b[::-1], bwd_c[::-1], dt_bwd[::-1], decay_rate
    )
    identity = (
        jnp.ones((heads,), jnp.float32),
        jnp.zeros((heads, head_size, state_size), jnp.float32),
    )
    fwd_in = entering_2(fwd_summary, "ctx", chain, identity, False)
    bwd_in = entering_2(bwd_summary, "ctx", chain, identity, True)
    y_fwd = finish(fwd_parts, fwd_in[1])
    y_bwd = finish(bwd_parts, bwd_in[1])[::-1]
    skip_cols = jnp.repeat(skip_gain, head_size)
    total = y_fwd + y_bwd + skip_cols[None, :] * inner.astype(jnp.float32)
    gated = total * jax.nn.silu(gate.astype(jnp.float32))
    scale = lax.rsqrt(jnp.mean(gated * gated, axis=-1, keepdims=True) + 1e-05)
    normed = (gated * scale * norm_gain[None, :]).astype(jnp.bfloat16)
    mixed = jnp.dot(
        normed,
        lax.all_gather(out_weight, ("fsdp", "ctx"), axis=1, tiled=True),
        preferred_element_type=jnp.float32,
    ).astype(jnp.bfloat16)
    return mixed[None]


def solution(mesh):
    in_specs = (
        P("fsdp", "ctx", None),
        P(None, ("fsdp", "ctx")),
        P(None, ("fsdp", "ctx")),
        P(),
        P(),
        P(),
        P(),
        P(None, ("fsdp", "ctx")),
    )
    out_specs = P("fsdp", "ctx", None)
    return jax.shard_map(shards, mesh=mesh, in_specs=in_specs, out_specs=out_specs, check_vma=False)
```

profile of v0, /device:TPU:1, one launch (start us, length us, event | category | flops | bytes accessed | tf_op | source)
XLA Modules:
  0.0 1759.5 jit_solution(7224074163287024116)
XLA Ops:
  14.6 405.2 %all-gather.17.cloned.1.call-done = bf16[256,2,2048]{2,1,0:T(2,128)(2,1)} async-done(((bf16[1,2,2048]{2,1,0:T(2,128)(2,1)}), bf16[256,2,2048]{2,1,0:T(2,128)(2,1)}) %all-gather.17.cloned.1.call-update) | async-done | bytes 2097168 | tf_op jit(solution)/shard_map/all_gather | solution.py:92
  419.8 2.7 reshape.102
  424.1 425.5 %all-gather.9.cloned.1.call-done = bf16[2048,4096]{0,1:T(8,128)(2,1)} async-done(((bf16[2048,16]{0,1:T(8,128)(2,1)}), bf16[2048,4096]{0,1:T(8,128)(2,1)}) %all-gather.9.cloned.1.call-update) | async-done | bytes 16777232 | tf_op jit(solution)/shard_map/all_gather | solution.py:91
  849.6 8.4 convolution_convert_fusion
  858.1 10.5 rev.21
  868.6 2.3 copy.64
  886.0 41.1 %all-gather.2 = f32[32,1,32]{2,1,0:T(1,128)S(1)} all-gather(f32[1,1,32]{2,1,0:T(1,128)} %get-tuple-element.269), channel_id=1, replica_groups=mesh['fsdp'=8,'ctx'=32] {'ctx'}, dimensions={0}, use_global_device_ids=true | all-gather | bytes 4224 | tf_op jit(solution)/shard_map/all_gather | solution.py:11
  930.7 38.8 %all-gather.1 = f32[32,1,32]{2,1,0:T(1,128)} all-gather(f32[1,1,32]{2,1,0:T(1,128)} %get-tuple-element.272), channel_id=1, replica_groups=mesh['fsdp'=8,'ctx'=32] {'ctx'}, dimensions={0}, use_global_device_ids=true | all-gather | bytes 4224 | tf_op jit(solution)/shard_map/all_gather | solution.py:11
  975.4 4.4 fusion.4
  979.9 3.3 fusion.3
  983.2 118.5 %all-gather.13.cloned.1.call-done = f32[32,32,64,128]{3,2,1,0:T(8,128)} async-done(((f32[1,32,64,128]{3,2,1,0:T(8,128)}), f32[32,32,64,128]{3,2,1,0:T(8,128)}) %all-gather.13.cloned.1.call-update) | async-done | bytes 33554448 | tf_op jit(solution)/shard_map/all_gather | solution.py:11
  1101.6 23.7 %rev.26 = f32[32,32,64,128]{3,2,1,0:T(8,128)} reverse(f32[32,32,64,128]{3,2,1,0:T(8,128)} %all-gather.13.cloned.1.call-done), dimensions={0} | reverse | bytes 67108864 | tf_op jit(solution)/shard_map/rev | solution.py:13
  1125.4 67.6 %while.29 = (s32[]{:T(128)}, f32[32,64,128]{2,1,0:T(8,128)S(1)}, s32[]{:T(128)}, f32[32,32]{1,0:T(8,128)}, f32[32,32,64,128]{3,2,1,0:T(8,128)}, /*index=5*/s32[]{:T(128)}, s32[]{:T(128)}) while((s32[]{:T(128)}, f32[32,64,128]{2,1,0:T(8,128)S(1)}, s32[]{:T(128)}, f32[32,32]{1,0:T(8,128)}, f32[32,32,64,128]{3,2,1,0:T(8,128)}, ...), condition=%wide.region_5.6_spmd.clone, body=%wide.region_4.5_spmd.clone.sunk | while | flops 1048580 | bytes 3146217 | solution.py:23
  1126.0 1.5 fusion.75
  1130.4 1.5 fusion.75
  1132.6 1.5 fusion.75
  1134.7 1.5 fusion.75
  1136.9 1.5 fusion.75
  1139.1 1.5 fusion.75
  1143.4 1.5 fusion.75
  1145.6 1.5 fusion.75
  1147.8 1.5 fusion.75
  1149.9 1.5 fusion.75
  1152.1 1.5 fusion.75
  1154.3 1.5 fusion.75
  1156.4 1.5 fusion.75
  1160.8 1.5 fusion.75
  1162.9 1.5 fusion.75
  1165.1 1.5 fusion.75
  1171.6 1.8 fusion.75
  1174.1 1.6 fusion.75
  1176.3 1.5 fusion.75
  1178.5 1.5 fusion.75
  1191.5 1.5 fusion.75
  1193.0 1.7 convert_bitcast_fusion
  1195.3 4.5 copy.82
  1199.8 3.6 reshape.112
  1203.4 10.5 rev.27
  1213.9 114.8 %all-gather.11.cloned.1.call-done = f32[32,32,64,128]{3,2,1,0:T(8,128)} async-done(((f32[1,32,64,128]{3,2,1,0:T(8,128)}), f32[32,32,64,128]{3,2,1,0:T(8,128)}) %all-gather.11.cloned.1.call-update) | async-done | bytes 33554448 | tf_op jit(solution)/shard_map/all_gather | solution.py:11
  1328.8 67.3 %while.28 = (s32[]{:T(128)}, f32[32,64,128]{2,1,0:T(8,128)S(1)}, s32[]{:T(128)}, f32[32,32]{1,0:T(8,128)}, f32[32,32,64,128]{3,2,1,0:T(8,128)}, /*index=5*/s32[]{:T(128)}, s32[]{:T(128)}) while((s32[]{:T(128)}, f32[32,64,128]{2,1,0:T(8,128)S(1)}, s32[]{:T(128)}, f32[32,32]{1,0:T(8,128)}, f32[32,32,64,128]{3,2,1,0:T(8,128)}, ...), condition=%wide.region_2.3_spmd.clone, body=%wide.region_1.2_spmd.clone.sunk | while | flops 1048580 | bytes 3146217 | solution.py:23
  1331.8 1.5 fusion.74
  1336.1 1.5 fusion.74
  1340.4 1.5 fusion.74
  1344.8 1.5 fusion.74
  1346.9 1.5 fusion.74
  1349.1 1.5 fusion.74
  1351.3 1.5 fusion.74
  1353.4 1.5 fusion.74
  1355.6 1.5 fusion.74
  1360.0 1.5 fusion.74
  1364.3 1.5 fusion.74
  1366.5 1.5 fusion.74
  1372.9 1.5 fusion.74
  1375.1 1.5 fusion.74
  1381.6 1.5 fusion.74
  1383.7 1.5 fusion.74
  1385.9 1.5 fusion.74
  1388.1 1.5 fusion.74
  1394.6 1.5 fusion.74
  1398.1 4.5 copy.81
  1402.6 3.6 reshape.111
  1406.2 4.5 multiply_reduce_fusion
  1410.7 334.8 %all-gather.15.cloned.1.call-done = bf16[2048,2048]{0,1:T(8,128)(2,1)} async-done(((bf16[2048,8]{0,1:T(8,128)(2,1)}), bf16[2048,2048]{0,1:T(8,128)(2,1)}) %all-gather.15.cloned.1.call-update) | async-done | bytes 8388624 | tf_op jit(solution)/shard_map/all_gather | solution.py:125
  1745.5 7.5 fusion.2
  (196 shorter events, 111.5 us)
Async XLA Ops:
  6.5 1.5 copy-start
  6.5 413.2 %all-gather.17.cloned.1.call-start = ((), (), s32[]{:S(2)}) async-start(), calls=%async_computation.4 | async-start | bytes 2105344 | tf_op jit(solution)/shard_map/all_gather | solution.py:92
  7.3 842.4 %all-gather.9.cloned.1.call-start = ((), (), s32[]{:S(2)}) async-start(), calls=%async_computation | async-start | bytes 16842752 | tf_op jit(solution)/shard_map/all_gather | solution.py:91
  8.0 1093.6 %all-gather.13.cloned.1.call-start = ((), (), s32[]{:S(2)}) async-start(), calls=%async_computation.2 | async-start | bytes 34603008 | tf_op jit(solution)/shard_map/all_gather | solution.py:11
  9.7 0.6 copy-start.16
  10.3 0.6 copy-start.15
  424.1 449.2 %copy-start.10 = (bf16[256,128]{1,0:T(8,128)(2,1)}, bf16[256,128]{1,0:T(8,128)(2,1)S(1)}, u32[]{:S(2)}) copy-start(bf16[256,128]{1,0:T(8,128)(2,1)S(1)} %rev.23) | copy-start | bytes 196612
  858.0 10.5 copy-start.5
  868.6 3.7 copy-start.17
  873.7 1.4 copy-start.4
  875.1 1.3 copy-start.14
  876.4 452.4 %all-gather.11.cloned.1.call-start = ((), (), s32[]{:S(2)}) async-start(), calls=%async_computation.1 | async-start | bytes 34603008 | tf_op jit(solution)/shard_map/all_gather | solution.py:11
  879.3 2.5 copy-start.12
  880.7 1.5 copy-start.6
  882.2 1.3 copy-start.2
  883.6 90.6 %copy-start.11 = (bf16[256,128]{1,0:T(8,128)(2,1)S(1)}, bf16[256,128]{1,0:T(8,128)(2,1)}, u32[]{:S(2)}) copy-start(bf16[256,128]{1,0:T(8,128)(2,1)} %copy-done.10) | copy-start | bytes 196612
  884.7 860.7 %all-gather.15.cloned.1.call-start = ((), (), s32[]{:S(2)}) async-start(), calls=%async_computation.3 | async-start | bytes 8421376 | tf_op jit(solution)/shard_map/all_gather | solution.py:125
  975.4 4.5 copy-start.7
  975.4 4.5 copy-start.18
  975.4 4.5 copy-start.19
  975.4 4.5 copy-start.20
  1125.3 67.6 %copy-start.22 = (f32[32]{0:T(128)S(1)}, f32[32]{0:T(128)}, u32[]{:S(2)}) copy-start(f32[32]{0:T(128)} %get-tuple-element.267) | copy-start | bytes 388
  1192.9 1.9 copy-start.9
  1328.8 67.3 %copy-start.3 = (f32[2,32,64,128]{3,2,1,0:T(8,128)S(1)}, f32[2,32,64,128]{3,2,1,0:T(8,128)}, u32[]{:S(2)}) copy-start(f32[2,32,64,128]{3,2,1,0:T(8,128)} %copy-done.2) | copy-start | bytes 6291460
  1328.8 67.3 %copy-start.21 = (f32[32]{0:T(128)S(1)}, f32[32]{0:T(128)}, u32[]{:S(2)}) copy-start(f32[32]{0:T(128)} %get-tuple-element.270) | copy-start | bytes 388
  1396.0 1.6 copy-start.8
  1396.0 1.6 copy-start.13
  1406.2 339.3 %copy-start.23 = (f32[2048]{0:T(1024)S(1)}, f32[2048]{0:T(1024)}, u32[]{:S(2)}) copy-start(f32[2048]{0:T(1024)} %param.18) | copy-start | bytes 24580
  1745.5 7.5 copy-start.1
Sparse Core Ops, SparseCore 0:
  9.2 410.4 all-gather.16
  421.7 427.8 all-gather.8
  876.5 225.0 all-gather.12
  1104.3 224.4 all-gather.10
  1330.5 414.9 all-gather.14
where the time goes:
time: 1770 us; the launch traced here: 1760 us
  waiting for transfers between devices  1400 us (79%)
  local copies, waits for them, and re-layouts  128 us (7%)
  other arithmetic  107 us (6%)
  blocking collectives  79.9 us (5%)
  matrix products  28.6 us (2%)
    all_gather x1, waiting for transfers between devices, shards(): lax.all_gather(zx_weight, ('fsdp', 'ctx'), axis=1, tiled=True)  426 us
    all_gather x1, waiting for transfers between devices, shards(): lax.all_gather(bc_weight, ('fsdp', 'ctx'), axis=1, tiled=True)  405 us
    all_gather x1, waiting for transfers between devices, shards(): lax.all_gather(out_weight, ('fsdp', 'ctx'), axis=1, tiled=True)  335 us
    all_gather x2, waiting for transfers between devices, entering_2(): pieces = jax.tree.map(lambda part: lax.all_gather(part, axis), value)  233 us
    select_n x62, other arithmetic, hop(): jnp.where(position < mine, new, old)  91 us
    all_gather x2, blocking collectives, entering_2(): pieces = jax.tree.map(lambda part: lax.all_gather(part, axis), value)  79.9 us
    mul x62, local copies, waits for them, and re-layouts, chain(): later[0][:, None, None] * earlier[1] + later[1]  42.8 us
  transfers between devices with their start and end apart: 5, of which 5 were waited for; matrix products, arithmetic and copies ran while one was open for 13% of the time, Pallas kernels for 0%

commit v1 on v0

v1 whole, which is shorter than its diff:
```python
import functools

import jax
import jax.numpy as jnp
from jax import lax
from jax.experimental import pallas as pl
from jax.experimental.pallas import tpu as pltpu
from jax.sharding import PartitionSpec as P

MESH = pl.DeviceIdType.MESH
F32 = jnp.float32
BF16 = jnp.bfloat16
BLOCK = 128
ROWS = 512
NBLK = ROWS // BLOCK
WIDE = 1024
VMEM_BYTES = 60 * 1024 * 1024


def coords():
    f = lax.axis_index("fsdp")
    c = lax.axis_index("ctx")
    y, xl = f // 2, f % 2
    z, xh, core = c // 4, (c // 2) % 2, c % 2
    return y, xl, z, xh, core


def dev(y, x, z, core):
    return (y * 2 + x % 2, z * 4 + (x // 2) * 2 + core)


def dot_nt(a, b):
    return lax.dot_general(a, b, (((1,), (1,)), ((), ())), preferred_element_type=F32)


def dot_tn(a, b):
    return lax.dot_general(a, b, (((0,), (0,)), ((), ())), preferred_element_type=F32)


def dot_nn(a, b):
    return lax.dot_general(a, b, (((1,), (0,)), ((), ())), preferred_element_type=F32)


def parts3(v):
    hi = v.astype(BF16)
    r = v - hi.astype(F32)
    mid = r.astype(BF16)
    lo = (r - mid.astype(F32)).astype(BF16)
    return hi, mid, lo


def wait_bytes(ref, sem):
    pltpu.make_async_copy(ref, ref, sem).wait()


class Spread:
    def __init__(self, view, slot, send, recv):
        self.view, self.slot, self.send, self.recv = view, slot, send, recv
        self.started = []

    def copy(self, half, sy, sx, to, index):
        ref = self.view(half, sy, sx)
        c = pltpu.make_async_remote_copy(
            src_ref=ref,
            dst_ref=ref,
            send_sem=self.send.at[half, index],
            recv_sem=self.recv.at[half, index],
            device_id=to,
            device_id_type=MESH,
        )
        c.start()
        self.started.append(c)

    def begin(self):
        y, xl, z, xh, core = coords()
        x = xh * 2 + xl
        for k in (1, 3, 2):
            self.copy(0, self.slot(y), x, dev((y + k) % 4, x, z, core), k - 1)
            self.copy(1, self.slot(y), x, dev(y, (x + k) % 4, z, core), k - 1)
        for k in (1, 3, 2):
            self.copy(0, self.slot(y), x, dev(y, (x + k) % 4, z, core), 3 * k)
            self.copy(1, self.slot(y), x, dev((y + k) % 4, x, z, core), 3 * k)

    def forward(self):
        y, xl, z, xh, core = coords()
        x = xh * 2 + xl
        for j in (1, 3, 2):
            sy = self.slot((y - j) % 4)
            wait_bytes(self.view(0, sy, x), self.recv.at[0, j - 1])
            for k in (1, 3, 2):
                self.copy(0, sy, x, dev(y, (x + k) % 4, z, core), 12 + 3 * (k - 1) + j - 1)
            sx = (x - j) % 4
            wait_bytes(self.view(1, self.slot(y), sx), self.recv.at[1, j - 1])
            for k in (1, 3, 2):
                self.copy(1, self.slot(y), sx, dev((y + k) % 4, x, z, core), 12 + 3 * (k - 1) + j - 1)

    def arrivals(self):
        y, xl, z, xh, core = coords()
        x = xh * 2 + xl
        for j in (0, 1, 3, 2):
            for k in (1, 3, 2):
                index = 3 * k if j == 0 else 12 + 3 * (k - 1) + j - 1
                sy, sx = self.slot((y - j) % 4), (x - k) % 4
                wait_bytes(self.view(0, sy, sx), self.recv.at[0, index])
                yield 0, sy, sx
                sy, sx = self.slot((y - k) % 4), (x - j) % 4
                wait_bytes(self.view(1, sy, sx), self.recv.at[1, index])
                yield 1, sy, sx

    def drain(self):
        for c in self.started:
            c.wait_send()


def gather_kernel(
    zx, bc, ow, tok, wz, wb, wo, xs,
    bcs, ows, bcm, bcf, owm, owf,
    zsend, zrecv, bsend, brecv, osend, orecv, local,
    gs, gr, swap_s, swap_r,
):
    y, xl, z, xh, core = coords()
    x = xh * 2 + xl
    h, zc = z // 4, z % 4
    t, zl = zc // 2, zc % 2
    inner, yy = y // 2, y % 2
    ys = yy + 2 * t
    y_to = yy + 2 * ((t + 1 + inner) % 2)

    barrier = pltpu.get_barrier_semaphore()
    count = 0
    for dz in range(8):
        for dc in range(2):
            for dy in (0, 2):
                if (dz, dc, dy) != (0, 0, 0):
                    to = dev((y + dy) % 4, x, (z + dz) % 8, (core + dc) % 2)
                    pl.semaphore_signal(barrier, inc=1, device_id=to, device_id_type=MESH)
                    count += 1
    for k in (1, 3):
        pl.semaphore_signal(barrier, inc=1, device_id=dev((y + k) % 4, x, z, core), device_id_type=MESH)
        count += 1
    for k in (1, 2, 3):
        pl.semaphore_signal(barrier, inc=1, device_id=dev(y, (x + k) % 4, z, core), device_id_type=MESH)
        count += 1
    pl.semaphore_wait(barrier, count)

    def first(src, dst, to_y, send, recv):
        is_self = jnp.logical_and(to_y == y, h == core)
        for dz in (0, 1, 7, 2, 6, 3, 5, 4):
            c = pltpu.make_async_remote_copy(
                src_ref=src,
                dst_ref=dst,
                send_sem=send.at[dz],
                recv_sem=recv,
                device_id=dev(to_y, x, (z + dz) % 8, h),
                device_id_type=MESH,
            )
            if dz:
                c.start()
            else:

                @pl.when(is_self)
                def _():
                    pltpu.make_async_copy(src, dst, recv).start()

                @pl.when(jnp.logical_not(is_self))
                def _():
                    c.start()

        def done():
            for dz in range(8):
                if dz:
                    wait_bytes(src, send.at[dz])
                else:

                    @pl.when(jnp.logical_not(is_self))
                    def _():
                        wait_bytes(src, send.at[0])

        return done

    def own_z(g, sy, sl, src_core):
        return wz.at[g, sy, xl, sl, xh, pl.ds(src_core * 16, 16)]

    dones = [
        first(bc, bcs.at[zc, core], y, bsend, brecv.at[zc, core]),
        first(zx, own_z(inner, ys, zl, core), y_to, zsend, zrecv.at[inner, zl, core]),
        first(ow, ows.at[zc, core], y, osend, orecv.at[zc, core]),
    ]
    partner = dev(y, x, z, 1 - core)
    tok_own = pltpu.make_async_copy(tok, xs.at[core], local.at[0])
    tok_own.start()
    tok_far = pltpu.make_async_remote_copy(
        src_ref=tok, dst_ref=xs.at[core], send_sem=swap_s.at[0], recv_sem=swap_r.at[0],
        device_id=partner, device_id_type=MESH,
    )
    tok_far.start()

    for q in range(4):
        for s in range(2):
            wait_bytes(bcs.at[q, s], brecv.at[q, s])
    for q in range(4):
        for s in range(2):
            v = bcs[q, s].astype(F32)
            for j in range(8):
                bcf[4 * q + 2 * s : 4 * q + 2 * s + 2, 256 * j : 256 * j + 256] = v[2 * j : 2 * j + 2, :]
    bcm[...] = bcf[...].astype(BF16)
    put = pltpu.make_async_copy(bcm, wb.at[y, core, xl, xh], local.at[1])
    put.start()
    put.wait()

    def view_b(half, sy, sx):
        return wb.at[sy, core, sx % 2, sx // 2, :, pl.ds(1024 * half, 1024)]

    def view_g(g):
        return lambda half, sy, sx: wz.at[g, sy, sx % 2, half, sx // 2]

    def view_o(half, sy, sx):
        return wo.at[sy, sx % 2, core, pl.ds(2 * half, 2), sx // 2]

    same = lambda v: v
    flip = lambda v: (v + 2) % 4
    set_b = Spread(view_b, same, gs.at[0], gr.at[0])
    set_i = Spread(view_g(1), same, gs.at[1], gr.at[1])
    set_g = Spread(view_g(0), flip, gs.at[2], gr.at[2])
    set_o = Spread(view_o, same, gs.at[3], gr.at[3])

    set_b.begin()
    for s in range(2):
        for r in range(2):
            wait_bytes(own_z(1, y, s, r), zrecv.at[1, s, r])
    set_i.begin()
    set_b.forward()
    set_i.forward()

    for q in range(4):
        for s in range(2):
            wait_bytes(ows.at[q, s], orecv.at[q, s])
    for q in range(4):
        for s in range(2):
            v = ows[q, s].astype(F32)
            for j in range(2):
                owf[q, 8 * s : 8 * s + 8, 1024 * j : 1024 * j + 1024] = v[8 * j : 8 * j + 8, :]
    owm[...] = owf[...].astype(BF16)
    put = pltpu.make_async_copy(owm, wo.at[y, xl, core, :, xh], local.at[2])
    put.start()
    put.wait()
    for s in range(2):
        for r in range(2):
            wait_bytes(own_z(0, flip(y), s, r), zrecv.at[0, s, r])

    def swap(ref, index):
        c = pltpu.make_async_remote_copy(
            src_ref=ref, dst_ref=ref, send_sem=swap_s.at[index], recv_sem=swap_r.at[index],
            device_id=partner, device_id_type=MESH,
        )
        c.start()
        return c

    set_g.begin()
    set_o.begin()
    for _ in set_b.arrivals():
        pass
    swaps = [swap(wb.at[:, core], 1)]
    for _ in set_i.arrivals():
        pass
    set_g.forward()
    set_o.forward()
    for _ in set_g.arrivals():
        pass
    for _ in set_o.arrivals():
        pass
    swaps.append(swap(wo.at[:, :, core], 2))

    for done in dones:
        done()
    for s in (set_b, set_i, set_g, set_o):
        s.drain()
    tok_own.wait()
    tok_far.wait_send()
    wait_bytes(xs.at[1 - core], swap_r.at[0])
    for c in swaps:
        c.wait_send()
    wait_bytes(wb.at[:, 1 - core], swap_r.at[1])
    wait_bytes(wo.at[:, :, 1 - core], swap_r.at[2])


ANY = pl.BlockSpec(memory_space=pl.ANY)
INV = pl.BlockSpec(memory_space=pltpu.VMEM)


def gather(zx, bc, ow, tok):
    dma = pltpu.SemaphoreType.DMA
    return pl.pallas_call(
        gather_kernel,
        out_shape=(
            jax.ShapeDtypeStruct((2, 4, 2, 2, 2, 32, 2048), BF16),
            jax.ShapeDtypeStruct((4, 2, 2, 2, 16, 2048), BF16),
            jax.ShapeDtypeStruct((4, 2, 2, 4, 2, 16, 2048), BF16),
            jax.ShapeDtypeStruct((2, 256, 2048), BF16),
        ),
        in_specs=[ANY] * 4,
        out_specs=(ANY,) * 4,
        scratch_shapes=[
            pltpu.VMEM((4, 2, 16, 256), BF16),
            pltpu.VMEM((4, 2, 16, 1024), BF16),
            pltpu.VMEM((16, 2048), BF16),
            pltpu.VMEM((16, 2048), F32),
            pltpu.VMEM((4, 16, 2048), BF16),
            pltpu.VMEM((4, 16, 2048), F32),
            dma((8,)), dma((2, 2, 2)),
            dma((8,)), dma((4, 2)),
            dma((8,)), dma((4, 2)),
            dma((3,)),
            dma((4, 2, 21)), dma((4, 2, 21)),
            dma((3,)), dma((3,)),
        ],
        compiler_params=pltpu.CompilerParams(
            collective_id=0, has_side_effects=True, vmem_limit_bytes=VMEM_BYTES
        ),
        name="gather",
    )(zx, bc, ow, tok)


def head_map(lane, shape, axis):
    i = lax.broadcasted_iota(jnp.int32, shape, axis)
    zl, xl, yy, t = i % 2, (i // 2) % 2, (i // 4) % 2, (i // 8) % 2
    return (yy * 2 + xl) * 8 + lane * 4 + t * 2 + zl


def natural(lane, g):
    y, xl = g // 2, g % 2
    yy, t = y % 2, y // 2
    return ((yy * 2 + xl) * 8 + lane * 4 + t * 2) * 64


def widen(v):
    stacked = jnp.concatenate(parts3(v), axis=1)
    r = lax.broadcasted_iota(jnp.int32, (48, WIDE), 0)
    c = lax.broadcasted_iota(jnp.int32, (48, WIDE), 1)
    spread = (r % 16 == c // 64).astype(BF16)
    return dot_nn(stacked, spread)


def scan_kernel(x, wi, wb, dtw, decay, skip, inner, bco, lamo, kst, dend, pay, yo, dts, lamt):
    core = lax.axis_index("ctx") % 2
    xv = x[...].reshape(ROWS, 2048)
    bco[...] = dot_nt(xv, wb[...].reshape(512, 2048)).astype(BF16)
    for g in range(4):
        w = wi[0, g].reshape(256, 2048)
        inner[:, 256 * g : 256 * g + 256] = dot_nt(xv, w).astype(BF16)
    raw = dot_nt(xv, dtw[...]).astype(BF16)
    row = lax.broadcasted_iota(jnp.int32, (64, 32), 0)
    col = lax.broadcasted_iota(jnp.int32, (64, 32), 1)
    pick = row == head_map(core, (64, 32), 1) + 32 * (col // 16)
    v = dot_nn(raw, pick.astype(BF16))
    dt = jnp.maximum(v, 0.0) + jnp.log1p(jnp.exp(-jnp.abs(v)))
    dts[...] = dt

    def choose(ref):
        one = (lax.broadcasted_iota(jnp.int32, (32, 16), 0) == head_map(core, (32, 16), 1)).astype(BF16)
        return sum(dot_nn(p, one) for p in parts3(ref[...]))

    rate = choose(decay)
    gain = widen(choose(skip))
    rates = jnp.concatenate([rate, rate], axis=1)[:1]
    step = -dt * rates
    logdt = jnp.log(dt)
    r = lax.broadcasted_iota(jnp.int32, (BLOCK, BLOCK), 0)
    c = lax.broadcasted_iota(jnp.int32, (BLOCK, BLOCK), 1)
    lower = (c <= r).astype(BF16)
    upper = (c >= r).astype(BF16)
    fwd_col = lax.broadcasted_iota(jnp.int32, (BLOCK, 32), 1) < 16
    for b in range(NBLK):
        rows = slice(b * BLOCK, b * BLOCK + BLOCK)
        ps = parts3(step[rows])
        lam = jnp.where(fwd_col, sum(dot_nn(lower, p) for p in ps), sum(dot_nn(upper, p) for p in ps))
        lamo[rows, :] = lam
        padded = jnp.concatenate([lam - logdt[rows], jnp.zeros((BLOCK, 96), F32)], axis=1)
        lamt[b] = jnp.transpose(padded)[:32]

    for d in range(2):
        cols = slice(16 * d, 16 * d + 16)
        state = jnp.zeros((BLOCK, WIDE), F32)
        decays = jnp.ones((1, WIDE), F32)
        for b in range(NBLK) if d == 0 else reversed(range(NBLK)):
            rows = slice(b * BLOCK, b * BLOCK + BLOCK)
            lam = lamo[rows, cols]
            end = lam[BLOCK - 1 : BLOCK] if d == 0 else lam[0:1]
            factor = jnp.exp(end - lam) * dts[rows, cols]
            scaled = (widen(factor) * inner[rows, :].astype(F32)).astype(BF16)
            k = dot_tn(bco[rows, 256 * d : 256 * d + 128], scaled)
            de = widen(jnp.broadcast_to(jnp.exp(end), (8, 16)))[:1]
            dend[d, b] = de
            kst[d, b] = k
            state = de * state + k
            decays = decays * de
        for j in range(16):
            q, nh = j // 2, j % 2
            pay[j, 64 * d : 64 * d + 64, :] = state[64 * nh : 64 * nh + 64, 128 * q : 128 * q + 128].astype(BF16)
        if d == 0:
            decay_rows = list(parts3(decays))
        else:
            decay_rows = decay_rows + list(parts3(decays))
    tail = jnp.concatenate([p.astype(F32) for p in decay_rows] + [jnp.zeros((10, WIDE), F32)], axis=0).astype(BF16)
    for j in range(16):
        q = j // 2
        pay[j, 128:144, :] = tail[:, 128 * q : 128 * q + 128]

    left = lax.broadcasted_iota(jnp.int32, (BLOCK, BLOCK), 1) < 64

    def block(b, carry):
        rows = pl.ds(pl.multiple_of(b * BLOCK, BLOCK), BLOCK)
        gf = dot_nt(bco[rows, 128:256], bco[rows, 0:128])
        gb = dot_nt(bco[rows, 384:512], bco[rows, 256:384])
        g = jnp.where(r > c, gf, jnp.where(r < c, gb, 0.0))
        lam = lamo[rows, :]
        lt = lamt[b]
        for q in range(8):
            ws = []
            for i in range(2):
                lh = 2 * q + i
                gap_f = lam[:, lh : lh + 1] - lt[lh : lh + 1, :]
                gap_b = lam[:, 16 + lh : 17 + lh] - lt[16 + lh : 17 + lh, :]
                ws.append((g * jnp.exp(jnp.where(r > c, gap_f, gap_b))).astype(BF16))
            pair = inner[rows, 128 * q : 128 * q + 128]
            zero = jnp.zeros_like(pair)
            stack = jnp.concatenate([jnp.where(left, pair, zero), jnp.where(left, zero, pair)], axis=0)
            out = dot_nn(jnp.concatenate(ws, axis=1), stack)
            yo[rows, 128 * q : 128 * q + 128] = out + gain[:1, 128 * q : 128 * q + 128] * pair.astype(F32)
        return carry

    lax.fori_loop(0, NBLK, block, 0)


def local_scan(x, wz, wb, dtw, decay, skip):
    sd = jax.ShapeDtypeStruct
    return pl.pallas_call(
        scan_kernel,
        out_shape=(
            sd((ROWS, WIDE), BF16),
            sd((ROWS, 512), BF16),
            sd((ROWS, 32), F32),
            sd((2, NBLK, BLOCK, WIDE), F32),
            sd((2, NBLK, 1, WIDE), F32),
            sd((16, 144, 128), BF16),
            sd((ROWS, WIDE), F32),
        ),
        grid=(1,),
        in_specs=[
            INV,
            pl.BlockSpec((1, 4, 2, 2, 2, 32, 2048), lambda i: (1, 0, 0, 0, 0, 0, 0)),
            INV, INV, INV, INV,
        ],
        out_specs=(INV,) * 7,
        scratch_shapes=[pltpu.VMEM((ROWS, 32), F32), pltpu.VMEM((NBLK, 32, BLOCK), F32)],
        compiler_params=pltpu.CompilerParams(vmem_limit_bytes=VMEM_BYTES),
        name="scan",
    )(x, wz, wb, dtw, decay, skip)


def states_kernel(pay, out, got, reply, s1, r1, s2, r2):
    y, xl, z, xh, core = coords()
    me = z * 2 + xh

    def at(j):
        return dev(y, (j % 2) * 2 + xl, j // 2, core)

    barrier = pltpu.get_barrier_semaphore()
    for k in range(1, 16):
        pl.semaphore_signal(barrier, inc=1, device_id=at((me + k) % 16), device_id_type=MESH)
    pl.semaphore_wait(barrier, 15)

    def send(src, dst, ss, rs):
        cs = []
        for k in range(1, 16):
            j = (me + k) % 16
            c = pltpu.make_async_remote_copy(
                src_ref=src.at[j], dst_ref=dst.at[me], send_sem=ss.at[k - 1], recv_sem=rs.at[k - 1],
                device_id=at(j), device_id_type=MESH,
            )
            c.start()
            cs.append(c)
        dst[pl.ds(me, 1)] = src[pl.ds(me, 1)]
        for k in range(1, 16):
            wait_bytes(dst.at[(me - k) % 16], rs.at[k - 1])
        return cs

    cs = send(pay, got, s1, r1)
    for d in range(2):
        state = jnp.zeros((64, 128), F32)
        for i in range(16) if d == 0 else reversed(range(16)):
            reply[i, 64 * d : 64 * d + 64, :] = state.astype(BF16)
            ds = got[i, 128:144, :].astype(F32)
            decay = ds[3 * d : 3 * d + 1] + ds[3 * d + 1 : 3 * d + 2] + ds[3 * d + 2 : 3 * d + 3]
            state = decay * state + got[i, 64 * d : 64 * d + 64, :].astype(F32)
    cs += send(reply, out, s2, r2)
    for c in cs:
        c.wait_send()


def exchange_states(pay):
    dma = pltpu.SemaphoreType.DMA
    return pl.pallas_call(
        states_kernel,
        out_shape=jax.ShapeDtypeStruct((16, 128, 128), BF16),
        in_specs=[INV],
        out_specs=INV,
        scratch_shapes=[
            pltpu.VMEM((16, 144, 128), BF16),
            pltpu.VMEM((16, 128, 128), BF16),
            dma((15,)), dma((15,)), dma((15,)), dma((15,)),
        ],
        compiler_params=pltpu.CompilerParams(
            collective_id=1, has_side_effects=True, vmem_limit_bytes=VMEM_BYTES
        ),
        name="states",
    )(pay)


def finish_kernel(x, wg, bco, lamo, kst, dend, ent, yo, gain, out, sq, enter):
    core = lax.axis_index("ctx") % 2
    for q in range(8):
        cols = slice(128 * q, 128 * q + 128)
        for nh in range(2):
            piece = ent[2 * q + nh].astype(F32)
            enter[0, 64 * nh : 64 * nh + 64, cols] = piece[:64]
            enter[1, 64 * nh : 64 * nh + 64, cols] = piece[64:]
    total = [None] * NBLK
    for d in range(2):
        state = enter[d]
        for b in range(NBLK) if d == 0 else reversed(range(NBLK)):
            rows = slice(b * BLOCK, b * BLOCK + BLOCK)
            cv = bco[rows, 256 * d + 128 : 256 * d + 256]
            y = widen(jnp.exp(lamo[rows, 16 * d : 16 * d + 16])) * dot_nn(cv, state.astype(BF16))
            yo[rows, :] = yo[rows, :] + y
            state = dend[d, b] * state + kst[d, b]
    xv = x[...].reshape(ROWS, 2048)
    squares = jnp.zeros((ROWS, 1), F32)
    for g in range(4):
        gate = dot_nt(xv, wg[0, g].reshape(256, 2048)).astype(BF16).astype(F32)
        gated = yo[:, 256 * g : 256 * g + 256] * (gate / (1.0 + jnp.exp(-gate)))
        squares = squares + jnp.sum(gated * gated, axis=1, keepdims=True)
        for i in range(2):
            base = pl.multiple_of(natural(core, 2 * g + i), 128)
            cols = slice(256 * g + 128 * i, 256 * g + 128 * i + 128)
            out[:, cols] = (gated[:, 128 * i : 128 * i + 128] * gain[0:1, pl.ds(base, 128)]).astype(BF16)
    sq[...] = jnp.broadcast_to(squares, (ROWS, 128))


def finish(x, wz, bco, lamo, kst, dend, ent, yo, gain):
    return pl.pallas_call(
        finish_kernel,
        out_shape=(jax.ShapeDtypeStruct((ROWS, WIDE), BF16), jax.ShapeDtypeStruct((ROWS, 128), F32)),
        grid=(1,),
        in_specs=[
            INV,
            pl.BlockSpec((1, 4, 2, 2, 2, 32, 2048), lambda i: (0, 0, 0, 0, 0, 0, 0)),
            INV, INV, INV, INV, INV, INV, INV,
        ],
        out_specs=(INV, INV),
        scratch_shapes=[pltpu.VMEM((2, BLOCK, WIDE), F32)],
        compiler_params=pltpu.CompilerParams(vmem_limit_bytes=VMEM_BYTES),
        name="finish",
    )(x, wz, bco, lamo, kst, dend, ent, yo, gain)


def pair_kernel(g, sq, wide, sqo, far, farsq, ss, rs):
    y, xl, z, xh, core = coords()
    partner = dev(y, xh * 2 + xl, z, 1 - core)
    barrier = pltpu.get_barrier_semaphore()
    pl.semaphore_signal(barrier, inc=1, device_id=partner, device_id_type=MESH)
    pl.semaphore_wait(barrier, 1)
    theirs = pl.ds(pl.multiple_of((1 - core) * 256, 256), 256)
    mine = pl.ds(pl.multiple_of(core * 256, 256), 256)
    cs = []
    for i, (src, dst) in enumerate(((g.at[theirs], far), (sq.at[theirs], farsq))):
        c = pltpu.make_async_remote_copy(
            src_ref=src, dst_ref=dst, send_sem=ss.at[i], recv_sem=rs.at[i],
            device_id=partner, device_id_type=MESH,
        )
        c.start()
        cs.append(c)
    for i in range(8):
        wide[:, pl.ds(pl.multiple_of(natural(core, i), 128), 128)] = g[mine, 128 * i : 128 * i + 128]
    for c in cs:
        c.wait()
    for i in range(8):
        wide[:, pl.ds(pl.multiple_of(natural(1 - core, i), 128), 128)] = far[:, 128 * i : 128 * i + 128]
    sqo[...] = sq[mine, :] + farsq[...]


def exchange_pair(g, sq):
    dma = pltpu.SemaphoreType.DMA
    return pl.pallas_call(
        pair_kernel,
        out_shape=(jax.ShapeDtypeStruct((256, 2048), BF16), jax.ShapeDtypeStruct((256, 128), F32)),
        in_specs=[INV, INV],
        out_specs=(INV, INV),
        scratch_shapes=[
            pltpu.VMEM((256, WIDE), BF16),
            pltpu.VMEM((256, 128), F32),
            dma((2,)), dma((2,)),
        ],
        compiler_params=pltpu.CompilerParams(
            collective_id=2, has_side_effects=True, vmem_limit_bytes=VMEM_BYTES
        ),
        name="pair",
    )(g, sq)


def out_kernel(g, sq, wo, out):
    scale = lax.rsqrt(sq[:, :1] * (1.0 / 2048.0) + 1e-05)
    out[...] = (dot_nt(g[...], wo[...].reshape(256, 2048)) * scale).astype(BF16)


def project_out(g, sq, wo):
    return pl.pallas_call(
        out_kernel,
        out_shape=jax.ShapeDtypeStruct((256, 2048), BF16),
        grid=(8,),
        in_specs=[
            pl.BlockSpec((256, 2048), lambda i: (0, 0)),
            pl.BlockSpec((256, 128), lambda i: (0, 0)),
            pl.BlockSpec((1, 1, 2, 4, 2, 16, 2048), lambda i: (i // 2, i % 2, 0, 0, 0, 0, 0)),
        ],
        out_specs=pl.BlockSpec((256, 256), lambda i: (0, i)),
        compiler_params=pltpu.CompilerParams(vmem_limit_bytes=VMEM_BYTES),
        name="project_out",
    )(g, sq, wo)


def shards(tokens, zx_weight, bc_weight, dt_weight, decay_rate, skip_gain, norm_gain, out_weight):
    zx = zx_weight.T
    bc = bc_weight.T.reshape(2, 8, 256).transpose(1, 0, 2).reshape(16, 256)
    ow = out_weight.T.reshape(8, 2, 1024).transpose(1, 0, 2).reshape(16, 1024)
    wz, wb, wo, xs = gather(zx, bc, ow, tokens[0])
    decay = jnp.broadcast_to(decay_rate[None], (8, 32))
    skip = jnp.broadcast_to(skip_gain[None], (8, 32))
    inner, bco, lam, kst, dend, pay, yo = local_scan(xs, wz, wb, dt_weight.T, decay, skip)
    ent = exchange_states(pay)
    g, sq = finish(xs, wz, bco, lam, kst, dend, ent, yo, norm_gain[None])
    wide, sqs = exchange_pair(g, sq)
    return project_out(wide, sqs, wo)[None]


def solution(mesh):
    columns = P(None, ("fsdp", "ctx"))
    in_specs = (P("fsdp", "ctx", None), columns, columns, P(), P(), P(), P(), columns)
    return jax.shard_map(
        shards, mesh=mesh, in_specs=in_specs, out_specs=P("fsdp", "ctx", None), check_vma=False
    )
```

time: 1770 us -> 209 us (0.12)
  waiting for transfers between devices: 1400 us -> 0 us
  Pallas kernels: 0 us -> 205 us
  local copies, waits for them, and re-layouts: 128 us -> 3.79 us
  other arithmetic: 107 us -> 0 us
  blocking collectives: 79.9 us -> 0 us
  matrix products: 28.6 us -> 0 us
    all_gather x5 -> x0, waiting for transfers between devices: 1400 us -> none  [the longest x1 426 us: shards(): lax.all_gather(zx_weight, ('fsdp', 'ctx'), axis=1, tiled=True)]
    pallas_call x0 -> x6, Pallas kernels: none -> 205 us  [the longest x1 125 us: gather(): pl.pallas_call(gather_kernel, out_shape=(jax.ShapeDtypeStruct((2, 4, 2, 2...]
    select_n x63 -> x0, other arithmetic: 91 us -> none  [the longest x62 91 us: hop(): jnp.where(position < mine, new, old)]
    all_gather x2 -> x0, blocking collectives: 79.9 us -> none  [entering_2(): pieces = jax.tree.map(lambda part: lax.all_gather(part, axis), value)]
    rev x8 -> x0, local copies, waits for them, and re-layouts: 48.7 us -> none  [the longest x2 24.3 us: entering_2(): pieces = jax.tree.map(lambda part: part[::-1], pieces)]
    mul x65 -> x0, local copies, waits for them, and re-layouts: 43.6 us -> none  [the longest x62 42.8 us: chain(): later[0][:, None, None] * earlier[1] + later[1]]
    dot_general x12 -> x0, matrix products: 28.6 us -> none  [the longest x2 9.16 us: project(): jnp.dot(token_rows, piece, preferred_element_type=jnp.float32)]
    reshape x10 -> x1, local copies, waits for them, and re-layouts: 19.1 us -> 1.3 us  [shards(): bc = bc_weight.T.reshape(2, 8, 256).transpose(1, 0, 2).reshape(16, 256)]
  transfers between devices with their start and end apart: 5 -> 0, of which waited for: 5 -> 0; matrix products, arithmetic and copies ran while one was open for 13% -> 0% of each run, Pallas kernels for 0% -> 0%
where the time goes in v1:
time: 209 us; the launch traced here: 208 us
  Pallas kernels  205 us (98%)
  local copies, waits for them, and re-layouts  3.79 us (2%)
    pallas_call x1, Pallas kernels, gather(): pl.pallas_call(gather_kernel, out_shape=(jax.ShapeDtypeStruct((2, 4, 2, 2...  125 us
    pallas_call x1, Pallas kernels, exchange_states(): pl.pallas_call(states_kernel, out_shape=jax.ShapeDtypeStruct((16, 128, 12...  36.4 us
    pallas_call x1, Pallas kernels, local_scan(): pl.pallas_call(scan_kernel, out_shape=(sd((ROWS, WIDE), BF16), sd((ROWS,...  17.3 us
    pallas_call x1, Pallas kernels, finish(): pl.pallas_call(finish_kernel, out_shape=(jax.ShapeDtypeStruct((ROWS, WIDE...  10.4 us
    pallas_call x1, Pallas kernels, project_out(): pl.pallas_call(out_kernel, out_shape=jax.ShapeDtypeStruct((256, 2048), BF...  8.82 us
    pallas_call x1, Pallas kernels, exchange_pair(): pl.pallas_call(pair_kernel, out_shape=(jax.ShapeDtypeStruct((256, 2048),...  6.39 us

profile of v1, /device:TPU:1, one launch (start us, length us, event | category | flops | bytes accessed | tf_op | source)
XLA Modules:
  0.0 208.4 jit_solution(6291876553252538696)
XLA Ops:
  0.0 1.2 broadcast_in_dim.8.decay
  1.3 1.2 broadcast_in_dim.9.skip
  2.5 1.3 reshape.15.bc
  3.8 125.2 %gather.1 = (bf16[2,4,2,2,2,32,2048]{6,5,4,3,2,1,0:T(8,128)(2,1)}, bf16[4,2,2,2,16,2048]{5,4,3,2,1,0:T(8,128)(2,1)}, bf16[4,2,2,4,2,16,2048]{6,5,4,3,2,1,0:T(8,128)(2,1)}, bf16[2,256,2048]{2,1,0:T(8,128)(2,1)}) custom-call(bf16[16,2048]{1,0:T(8,128)(2,1)} %bitcast.19, bf16[16,256]{1,0:T(8,128)(2,1)} %reshape.15.bc, bf16[16,1024]{1,0:T(8,128)(2,1)} %bitcast.20, ...), custom_call_target="tpu_custom_call" | custom-call | tf_op jit(solution)/shard_map/gather/pallas_call | solution.py:293
  129.0 17.3 %scan.1 = (bf16[512,1024]{1,0:T(8,128)(2,1)}, bf16[512,512]{1,0:T(8,128)(2,1)}, f32[512,32]{1,0:T(8,128)}, f32[2,4,128,1024]{3,2,1,0:T(8,128)}, f32[2,4,1,1024]{...) custom-call(bf16[2,256,2048]{2,1,0:T(8,128)(2,1)} %get-tuple-element.19.x, ...), custom_call_target="tpu_custom_call" | custom-call | tf_op jit(solution)/shard_map/scan/pallas_call | solution.py:437
  146.3 36.4 %states.1.ent = bf16[16,128,128]{2,1,0:T(8,128)(2,1)} custom-call(bf16[16,144,128]{2,1,0:T(8,128)(2,1)} %get-tuple-element.26.pay), custom_call_target="tpu_custom_call" | custom-call | tf_op jit(solution)/shard_map/states/pallas_call | solution.py:503
  182.8 10.4 %finish.1 = (bf16[512,1024]{1,0:T(8,128)(2,1)}, f32[512,128]{1,0:T(8,128)}) custom-call(bf16[2,256,2048]{2,1,0:T(8,128)(2,1)} %get-tuple-element.19.x, bf16[2,4,2,2,2,32,2048]{6,5,4,3,2,1,0:T(8,128)(2,1)} %get-tuple-element.20.wi.wg, bf16[512,512]{1,0:T(8,128)(2,1)} %get-tuple-element.22.bco, f32[512,32]{1,0:T(8,128)} %get-tuple-element.23.lamo, ...), custom_call_target="tpu_custom_call" | custom-call | tf_op jit(solution)/shard_map/finish/pallas_call | solution.py:551
  193.2 6.4 %pair.1 = (bf16[256,2048]{1,0:T(8,128)(2,1)}, f32[256,128]{1,0:T(8,128)}) custom-call(bf16[512,1024]{1,0:T(8,128)(2,1)} %get-tuple-element.28.g, f32[512,128]{1,0:T(8,128)} %get-tuple-element.29.sq), custom_call_target="tpu_custom_call" | custom-call | tf_op jit(solution)/shard_map/pair/pallas_call | solution.py:594
  199.6 8.8 %project_out.1 = bf16[256,2048]{1,0:T(8,128)(2,1)} custom-call(bf16[256,2048]{1,0:T(8,128)(2,1)} %get-tuple-element.30.g, f32[256,128]{1,0:T(8,128)} %get-tuple-element.31.sq, bf16[4,2,2,4,2,16,2048]{6,5,4,3,2,1,0:T(8,128)(2,1)} %get-tuple-element.32.wo), custom_call_target="tpu_custom_call" | custom-call | tf_op jit(solution)/shard_map/project_out/pallas_call | solution.py:617

commit v2 on v0

v2 whole, which is shorter than its diff:
```python
import functools

import jax
import jax.numpy as jnp
from jax import lax
from jax.experimental import pallas as pl
from jax.experimental.pallas import tpu as pltpu
from jax.sharding import PartitionSpec as P

MESH = pl.DeviceIdType.MESH
F32 = jnp.float32
BF16 = jnp.bfloat16
BLOCK = 128
ROWS = 512
NBLK = ROWS // BLOCK
WIDE = 1024
VMEM_BYTES = 60 * 1024 * 1024


def coords():
    f = lax.axis_index("fsdp")
    c = lax.axis_index("ctx")
    y, xl = f // 2, f % 2
    z, xh, core = c // 4, (c // 2) % 2, c % 2
    return y, xl, z, xh, core


def dev(y, x, z, core):
    return (y * 2 + x % 2, z * 4 + (x // 2) * 2 + core)


def dot_nt(a, b):
    return lax.dot_general(a, b, (((1,), (1,)), ((), ())), preferred_element_type=F32)


def dot_tn(a, b):
    return lax.dot_general(a, b, (((0,), (0,)), ((), ())), preferred_element_type=F32)


def dot_nn(a, b):
    return lax.dot_general(a, b, (((1,), (0,)), ((), ())), preferred_element_type=F32)


def parts3(v):
    hi = v.astype(BF16)
    r = v - hi.astype(F32)
    mid = r.astype(BF16)
    lo = (r - mid.astype(F32)).astype(BF16)
    return hi, mid, lo


def wait_bytes(ref, sem):
    pltpu.make_async_copy(ref, ref, sem).wait()


class Ring:
    def __init__(self, view, slot, send, recv):
        self.view, self.slot, self.send, self.recv = view, slot, send, recv
        self.started = []

    def ref(self, half, j, m, part=None):
        y, xl, z, xh, core = coords()
        x = xh * 2 + xl
        dy, dx = (j, m) if half == 0 else (m, j)
        return self.view(half, self.slot((y - dy) % 4), (x - dx) % 4, part)

    def copy(self, half, ref, axis, step, index):
        y, xl, z, xh, core = coords()
        x = xh * 2 + xl
        to = dev((y + step) % 4, x, z, core) if axis == half else dev(y, (x + step) % 4, z, core)
        c = pltpu.make_async_remote_copy(
            src_ref=ref, dst_ref=ref, send_sem=self.send.at[half, index], recv_sem=self.recv.at[half, index],
            device_id=to, device_id_type=MESH,
        )
        c.start()
        self.started.append(c)

    def wait(self, half, ref, index):
        wait_bytes(ref, self.recv.at[half, index])

    def both(self, half, j):
        ref = self.ref(half, j, 0)
        self.copy(half, ref, 1, 1, 4 + 4 * j)
        self.copy(half, ref, 1, 3, 5 + 4 * j)

    def begin(self):
        for half in range(2):
            ref = self.ref(half, 0, 0)
            self.copy(half, ref, 0, 1, 0)
            self.copy(half, ref, 0, 3, 1)
        for half in range(2):
            self.both(half, 0)

    def turn(self, half, axis, base, block):
        self.wait(half, block(1), base)
        self.copy(half, block(1, 0), axis, 1, base + 2)
        self.wait(half, block(3), base + 1)
        self.copy(half, block(3, 1), axis, 3, base + 3)

    def first(self):
        for half in range(2):
            self.turn(half, 0, 0, lambda n, part=None: self.ref(half, n, 0, part))
        for half in range(2):
            self.both(half, 1)
            self.both(half, 3)

    def second(self):
        for half in range(2):
            for part in range(2):
                self.wait(half, self.ref(half, 2, 0, part), 2 + part)
            self.both(half, 2)

    def third(self, j):
        for half in range(2):
            self.turn(half, 1, 4 + 4 * j, lambda n, part=None: self.ref(half, j, n, part))

    def fourth(self, j):
        for half in range(2):
            for part in range(2):
                self.wait(half, self.ref(half, j, 2, part), 6 + 4 * j + part)

    def drain(self):
        for c in self.started:
            c.wait_send()


def head_map(lane, shape, axis):
    i = lax.broadcasted_iota(jnp.int32, shape, axis)
    zl, xl, yy, t = i % 2, (i // 2) % 2, (i // 4) % 2, (i // 8) % 2
    return (yy * 2 + xl) * 8 + lane * 4 + t * 2 + zl


def natural(lane, g):
    y, xl = g // 2, g % 2
    yy, t = y % 2, y // 2
    return pl.multiple_of(((yy * 2 + xl) * 8 + lane * 4 + t * 2) * 64, 128)


def widen(v):
    stacked = jnp.concatenate(parts3(v), axis=1)
    r = lax.broadcasted_iota(jnp.int32, (48, WIDE), 0)
    c = lax.broadcasted_iota(jnp.int32, (48, WIDE), 1)
    spread = (r % 16 == c // 64).astype(BF16)
    return dot_nn(stacked, spread)


def kernel(
    zx, bc, ow, tok, dtw, decay, skip, gain, result,
    wz, wb, wo, xs, bst, bstf, bcs, ows, bcm, bcf, owm, owf,
    inner, bco, lams, dts, lamt, wide_f, wide_l, wm, kst, dend, yo, enter,
    pay, got, reply, ent, gbuf, wide, sqb, sqf,
    zsend, zrecv, bsend, brecv, osend, orecv, local,
    gs, gr, swap_s, swap_r, s1, r1, s2, r2, ps, pr,
):
    y, xl, z, xh, core = coords()
    x = xh * 2 + xl
    h, zc = z // 4, z % 4
    t, zl = zc // 2, zc % 2
    inner_side, yy = y // 2, y % 2
    ys = yy + 2 * t
    y_to = yy + 2 * ((t + 1 + inner_side) % 2)
    chip = z * 2 + xh
    partner = dev(y, x, z, 1 - core)

    def state_peer(j):
        return dev(y, (j % 2) * 2 + xl, j // 2, core)

    def remote(src, dst, ss, rs, to):
        return pltpu.make_async_remote_copy(
            src_ref=src, dst_ref=dst, send_sem=ss, recv_sem=rs, device_id=to, device_id_type=MESH
        )

    barrier = pltpu.get_barrier_semaphore()
    peers = []
    for dz in range(8):
        for dc in range(2):
            for dy in (0, 2):
                if (dz, dc, dy) != (0, 0, 0):
                    peers.append(dev((y + dy) % 4, x, (z + dz) % 8, (core + dc) % 2))
        peers.append(dev(y, (x + 2) % 4, (z + dz) % 8, core))
    for k in (1, 3):
        peers.append(dev((y + k) % 4, x, z, core))
        peers.append(dev(y, (x + k) % 4, z, core))
    for to in peers:
        pl.semaphore_signal(barrier, inc=1, device_id=to, device_id_type=MESH)
    for j in range(8):
        bstf[2 * j : 2 * j + 2, :] = bc[:, 256 * j : 256 * j + 256].astype(F32)
    bst[...] = bstf[...].astype(BF16)
    pl.semaphore_wait(barrier, len(peers))

    def first(src, dst, to_y, send, recv):
        is_self = jnp.logical_and(to_y == y, h == core)
        for dz in (0, 1, 7, 2, 6, 3, 5, 4):
            c = remote(src, dst, send.at[dz], recv, dev(to_y, x, (z + dz) % 8, h))
            if dz:
                c.start()
            else:

                @pl.when(is_self)
                def _():
                    pltpu.make_async_copy(src, dst, recv).start()

                @pl.when(jnp.logical_not(is_self))
                def _():
                    c.start()

        def done():
            for dz in range(8):
                if dz:
                    wait_bytes(src, send.at[dz])
                else:

                    @pl.when(jnp.logical_not(is_self))
                    def _():
                        wait_bytes(src, send.at[0])

        return done

    def own_z(g, sy, sl, src_core):
        return wz.at[g, sy, xl, sl, xh, pl.ds(src_core * 16, 16)]

    dones = [
        first(bst, bcs.at[zc, core], y, bsend, brecv.at[zc, core]),
        first(zx, own_z(inner_side, ys, zl, core), y_to, zsend, zrecv.at[inner_side, zl, core]),
    ]
    tok_own = pltpu.make_async_copy(tok, xs.at[core], local.at[0])
    tok_own.start()
    tok_far = remote(tok, xs.at[core], swap_s.at[0], swap_r.at[0], partner)
    tok_far.start()
    dones.append(first(ow, ows.at[zc, core], y, osend, orecv.at[zc, core]))

    def view_b(half, sy, sx, part):
        lanes = pl.ds(1024 * half, 1024) if part is None else pl.ds(1024 * half + 512 * part, 512)
        return wb.at[sy, core, sx % 2, sx // 2, :, lanes]

    def view_g(g):
        def view(half, sy, sx, part):
            rows = pl.ds(0, 32) if part is None else pl.ds(16 * part, 16)
            return wz.at[g, sy, sx % 2, half, sx // 2, rows]

        return view

    def view_o(half, sy, sx, part):
        tiles = pl.ds(2 * half, 2) if part is None else pl.ds(2 * half + part, 1)
        return wo.at[sy, sx % 2, core, tiles, sx // 2]

    same = lambda v: v
    flip = lambda v: (v + 2) % 4
    set_b = Ring(view_b, same, gs.at[0], gr.at[0])
    set_i = Ring(view_g(1), same, gs.at[1], gr.at[1])
    set_g = Ring(view_g(0), flip, gs.at[2], gr.at[2])
    set_o = Ring(view_o, same, gs.at[3], gr.at[3])

    for q in range(4):
        for s in range(2):
            wait_bytes(bcs.at[q, s], brecv.at[q, s])
    for q in range(4):
        for s in range(2):
            v = bcs[q, s].astype(F32)
            for j in range(8):
                bcf[4 * q + 2 * s : 4 * q + 2 * s + 2, 256 * j : 256 * j + 256] = v[2 * j : 2 * j + 2, :]
    bcm[...] = bcf[...].astype(BF16)
    put = pltpu.make_async_copy(bcm, wb.at[y, core, xl, xh], local.at[1])
    put.start()
    put.wait()
    set_b.begin()
    for s in range(2):
        for r in range(2):
            wait_bytes(own_z(1, y, s, r), zrecv.at[1, s, r])
    set_i.begin()
    set_b.first()
    set_i.first()
    set_b.second()
    set_i.second()

    tok_own.wait()
    wait_bytes(xs.at[1 - core], swap_r.at[0])
    raw = dot_nt(xs[...].reshape(ROWS, 2048), dtw[...]).astype(BF16)
    row = lax.broadcasted_iota(jnp.int32, (64, 32), 0)
    col = lax.broadcasted_iota(jnp.int32, (64, 32), 1)
    pick = row == head_map(core, (64, 32), 1) + 32 * (col // 16)
    v = dot_nn(raw, pick.astype(BF16))
    dt = jnp.maximum(v, 0.0) + jnp.log1p(jnp.exp(-jnp.abs(v)))
    dts[...] = dt

    set_b.third(0)
    set_i.third(0)

    def choose(ref):
        one = (lax.broadcasted_iota(jnp.int32, (32, 16), 0) == head_map(core, (32, 16), 1)).astype(BF16)
        wide_ref = jnp.broadcast_to(ref[...], (8, 32))
        return sum(dot_nn(p, one) for p in parts3(wide_ref))

    rate = choose(decay)
    skips = widen(choose(skip))
    rates = jnp.concatenate([rate, rate], axis=1)[:1]
    step = -dt * rates
    logdt = jnp.log(dt)
    r = lax.broadcasted_iota(jnp.int32, (BLOCK, BLOCK), 0)
    c = lax.broadcasted_iota(jnp.int32, (BLOCK, BLOCK), 1)
    lower = (c <= r).astype(BF16)
    upper = (c >= r).astype(BF16)
    fwd_col = lax.broadcasted_iota(jnp.int32, (BLOCK, 32), 1) < 16
    for b in range(NBLK):
        rows = slice(b * BLOCK, b * BLOCK + BLOCK)
        sp = parts3(step[rows])
        lam = jnp.where(fwd_col, sum(dot_nn(lower, p) for p in sp), sum(dot_nn(upper, p) for p in sp))
        lams[rows, :] = lam
        padded = jnp.concatenate([lam - logdt[rows], jnp.zeros((BLOCK, 96), F32)], axis=1)
        lamt[b] = jnp.transpose(padded)[:32]

    set_b.third(1)
    set_b.third(3)
    set_i.third(1)
    set_i.third(3)
    set_b.third(2)
    set_i.third(2)
    for j in range(4):
        set_b.fourth(j)
    swaps = [remote(wb.at[:, core], wb.at[:, core], swap_s.at[1], swap_r.at[1], partner)]
    swaps[0].start()

    for d in range(2):
        cols = slice(16 * d, 16 * d + 16)
        for b in range(NBLK):
            rows = slice(b * BLOCK, b * BLOCK + BLOCK)
            lam = lams[rows, cols]
            end = lam[BLOCK - 1 : BLOCK] if d == 0 else lam[0:1]
            wide_f[d, rows, :] = widen(jnp.exp(end - lam) * dts[rows, cols])
            wl = widen(jnp.exp(lam))
            wide_l[d, rows, :] = wl
            dend[d, b] = wl[BLOCK - 1 : BLOCK] if d == 0 else wl[0:1]

    wait_bytes(wb.at[:, 1 - core], swap_r.at[1])
    bco[...] = dot_nt(xs[...].reshape(ROWS, 2048), wb[...].reshape(512, 2048)).astype(BF16)

    def block_weights(b, carry):
        rows = pl.ds(pl.multiple_of(b * BLOCK, BLOCK), BLOCK)
        gf = dot_nt(bco[rows, 128:256], bco[rows, 0:128])
        gb = dot_nt(bco[rows, 384:512], bco[rows, 256:384])
        g = jnp.where(r > c, gf, jnp.where(r < c, gb, 0.0))
        lam = lams[rows, :]
        lt = lamt[b]
        for lh in range(16):
            gap_f = lam[:, lh : lh + 1] - lt[lh : lh + 1, :]
            gap_b = lam[:, 16 + lh : 17 + lh] - lt[16 + lh : 17 + lh, :]
            w = g * jnp.exp(jnp.where(r > c, gap_f, gap_b))
            wm[b, :, 128 * lh : 128 * lh + 128] = w.astype(BF16)
        return carry

    lax.fori_loop(0, NBLK, block_weights, 0)

    for j in range(4):
        set_i.fourth(j)
    for q in range(4):
        for s in range(2):
            wait_bytes(ows.at[q, s], orecv.at[q, s])
    for q in range(4):
        for s in range(2):
            v = ows[q, s].astype(F32)
            for j in range(2):
                owf[q, 8 * s : 8 * s + 8, 1024 * j : 1024 * j + 1024] = v[8 * j : 8 * j + 8, :]
    owm[...] = owf[...].astype(BF16)
    put = pltpu.make_async_copy(owm, wo.at[y, xl, core, :, xh], local.at[2])
    put.start()
    for s in range(2):
        for q in range(2):
            wait_bytes(own_z(0, flip(y), s, q), zrecv.at[0, s, q])
    set_g.begin()
    put.wait()
    set_o.begin()

    for g in range(4):
        w = wz[1, g].reshape(256, 2048)
        inner[:, 256 * g : 256 * g + 256] = dot_nt(xs[...].reshape(ROWS, 2048), w).astype(BF16)

    decay_rows = []
    for d in range(2):
        state = jnp.zeros((BLOCK, WIDE), F32)
        decays = jnp.ones((1, WIDE), F32)
        for b in range(NBLK) if d == 0 else reversed(range(NBLK)):
            rows = slice(b * BLOCK, b * BLOCK + BLOCK)
            scaled = (wide_f[d, rows, :] * inner[rows, :].astype(F32)).astype(BF16)
            k = dot_tn(bco[rows, 256 * d : 256 * d + 128], scaled)
            de = dend[d, b]
            kst[d, b] = k
            state = de * state + k
            decays = decays * de
        for j in range(16):
            q, nh = j // 2, j % 2
            pay[j, 64 * d : 64 * d + 64, :] = state[64 * nh : 64 * nh + 64, 128 * q : 128 * q + 128].astype(BF16)
        decay_rows += list(parts3(decays))
    tail = jnp.concatenate([p.astype(F32) for p in decay_rows] + [jnp.zeros((10, WIDE), F32)], axis=0).astype(BF16)
    for j in range(16):
        q = j // 2
        pay[j, 128:144, :] = tail[:, 128 * q : 128 * q + 128]

    def send_states(src, dst, ss, rs):
        cs = []
        for k in range(1, 16):
            j = (chip + k) % 16
            c = remote(src.at[j], dst.at[chip], ss.at[k - 1], rs.at[k - 1], state_peer(j))
            c.start()
            cs.append(c)
        dst[pl.ds(chip, 1)] = src[pl.ds(chip, 1)]
        return cs

    def wait_states(dst, rs):
        for k in range(1, 16):
            wait_bytes(dst.at[(chip - k) % 16], rs.at[k - 1])

    state_copies = send_states(pay, got, s1, r1)
    set_g.first()
    set_o.first()

    left = lax.broadcasted_iota(jnp.int32, (BLOCK, BLOCK), 1) < 64

    def block_intra(b, carry):
        rows = pl.ds(pl.multiple_of(b * BLOCK, BLOCK), BLOCK)
        for q in range(8):
            pair = inner[rows, 128 * q : 128 * q + 128]
            zero = jnp.zeros_like(pair)
            stack = jnp.concatenate([jnp.where(left, pair, zero), jnp.where(left, zero, pair)], axis=0)
            out = dot_nn(wm[b, :, 256 * q : 256 * q + 256], stack)
            yo[rows, 128 * q : 128 * q + 128] = out + skips[:1, 128 * q : 128 * q + 128] * pair.astype(F32)
        return carry

    lax.fori_loop(0, NBLK, block_intra, 0)

    set_g.second()
    set_o.second()
    wait_states(got, r1)
    for d in range(2):
        state = jnp.zeros((64, 128), F32)
        for i in range(16) if d == 0 else reversed(range(16)):
            reply[i, 64 * d : 64 * d + 64, :] = state.astype(BF16)
            ds = got[i, 128:144, :].astype(F32)
            de = ds[3 * d : 3 * d + 1] + ds[3 * d + 1 : 3 * d + 2] + ds[3 * d + 2 : 3 * d + 3]
            state = de * state + got[i, 64 * d : 64 * d + 64, :].astype(F32)
    state_copies += send_states(reply, ent, s2, r2)

    for j in (0, 1, 3, 2):
        set_g.third(j)
        set_o.third(j)
    wait_states(ent, r2)
    for q in range(8):
        cols = slice(128 * q, 128 * q + 128)
        for nh in range(2):
            piece = ent[2 * q + nh].astype(F32)
            enter[0, 64 * nh : 64 * nh + 64, cols] = piece[:64]
            enter[1, 64 * nh : 64 * nh + 64, cols] = piece[64:]
    for d in range(2):
        state = enter[d]
        for b in range(NBLK) if d == 0 else reversed(range(NBLK)):
            rows = slice(b * BLOCK, b * BLOCK + BLOCK)
            cv = bco[rows, 256 * d + 128 : 256 * d + 256]
            yo[rows, :] = yo[rows, :] + wide_l[d, rows, :] * dot_nn(cv, state.astype(BF16))
            state = dend[d, b] * state + kst[d, b]

    for j in range(4):
        set_g.fourth(j)
    theirs = pl.ds(pl.multiple_of((1 - core) * 256, 256), 256)
    mine = pl.ds(pl.multiple_of(core * 256, 256), 256)
    squares = jnp.zeros((ROWS, 1), F32)
    pair_copies = []
    for g in range(4):
        w = wz[0, g].reshape(256, 2048)
        gate = dot_nt(xs[...].reshape(ROWS, 2048), w).astype(BF16).astype(F32)
        gated = yo[:, 256 * g : 256 * g + 256] * (gate / (1.0 + jnp.exp(-gate)))
        squares = squares + jnp.sum(gated * gated, axis=1, keepdims=True)
        for i in range(2 * g, 2 * g + 2):
            place = pl.ds(natural(core, i), 128)
            cols = slice(128 * i, 128 * i + 128)
            part = gated[:, 128 * (i % 2) : 128 * (i % 2) + 128]
            gbuf[:, cols] = (part * gain[0:1, place]).astype(BF16)
            cp = remote(gbuf.at[theirs, cols], wide.at[:, place], ps.at[i], pr.at[i], partner)
            cp.start()
            pair_copies.append(cp)
            wide[:, place] = gbuf[mine, cols]
    sqb[...] = jnp.broadcast_to(squares, (ROWS, 128))
    cp = remote(sqb.at[theirs], sqf, ps.at[8], pr.at[8], partner)
    cp.start()
    pair_copies.append(cp)

    for j in range(4):
        set_o.fourth(j)
    swaps.append(remote(wo.at[:, :, core], wo.at[:, :, core], swap_s.at[2], swap_r.at[2], partner))
    swaps[1].start()
    for i in range(8):
        wait_bytes(wide.at[:, pl.ds(natural(1 - core, i), 128)], pr.at[i])
    wait_bytes(sqf, pr.at[8])
    scale = lax.rsqrt((sqb[mine, :1] + sqf[:, :1]) * (1.0 / 2048.0) + 1e-05)
    wait_bytes(wo.at[:, :, 1 - core], swap_r.at[2])
    for g in range(8):
        w = wo[g // 2, g % 2].reshape(256, 2048)
        result[:, 256 * g : 256 * g + 256] = (dot_nt(wide[...], w) * scale).astype(BF16)

    for done in dones:
        done()
    for s in (set_b, set_i, set_g, set_o):
        s.drain()
    tok_far.wait_send()
    for cp in swaps + state_copies + pair_copies:
        cp.wait_send()


ANY = pl.BlockSpec(memory_space=pl.ANY)
INV = pl.BlockSpec(memory_space=pltpu.VMEM)


def layer(zx, bc, ow, tok, dtw, decay, skip, gain):
    dma = pltpu.SemaphoreType.DMA
    vm = pltpu.VMEM
    return pl.pallas_call(
        kernel,
        out_shape=jax.ShapeDtypeStruct((256, 2048), BF16),
        in_specs=[ANY, INV, ANY, ANY, INV, INV, INV, INV],
        out_specs=INV,
        scratch_shapes=[
            vm((2, 4, 2, 2, 2, 32, 2048), BF16), vm((4, 2, 2, 2, 16, 2048), BF16),
            vm((4, 2, 2, 4, 2, 16, 2048), BF16), vm((2, 256, 2048), BF16),
            vm((16, 256), BF16), vm((16, 256), F32),
            vm((4, 2, 16, 256), BF16), vm((4, 2, 16, 1024), BF16),
            vm((16, 2048), BF16), vm((16, 2048), F32), vm((4, 16, 2048), BF16), vm((4, 16, 2048), F32),
            vm((ROWS, WIDE), BF16), vm((ROWS, 512), BF16), vm((ROWS, 32), F32), vm((ROWS, 32), F32),
            vm((NBLK, 32, BLOCK), F32), vm((2, ROWS, WIDE), F32), vm((2, ROWS, WIDE), F32),
            vm((NBLK, BLOCK, 2048), BF16), vm((2, NBLK, BLOCK, WIDE), F32), vm((2, NBLK, 1, WIDE), F32),
            vm((ROWS, WIDE), F32), vm((2, BLOCK, WIDE), F32),
            vm((16, 144, 128), BF16), vm((16, 144, 128), BF16), vm((16, 128, 128), BF16),
            vm((16, 128, 128), BF16), vm((ROWS, WIDE), BF16), vm((256, 2048), BF16),
            vm((ROWS, 128), F32), vm((256, 128), F32),
            dma((8,)), dma((2, 2, 2)), dma((8,)), dma((4, 2)), dma((8,)), dma((4, 2)), dma((3,)),
            dma((4, 2, 20)), dma((4, 2, 20)), dma((3,)), dma((3,)),
            dma((15,)), dma((15,)), dma((15,)), dma((15,)), dma((9,)), dma((9,)),
        ],
        compiler_params=pltpu.CompilerParams(
            collective_id=0, has_side_effects=True, vmem_limit_bytes=VMEM_BYTES
        ),
        name="layer",
    )(zx, bc, ow, tok, dtw, decay, skip, gain)


def shards(tokens, zx_weight, bc_weight, dt_weight, decay_rate, skip_gain, norm_gain, out_weight):
    ow = out_weight.T.reshape(8, 2, 1024).transpose(1, 0, 2).reshape(16, 1024)
    return layer(
        zx_weight.T, bc_weight.T, ow, tokens[0], dt_weight.T,
        decay_rate[None], skip_gain[None], norm_gain[None],
    )[None]


def solution(mesh):
    columns = P(None, ("fsdp", "ctx"))
    in_specs = (P("fsdp", "ctx", None), columns, columns, P(), P(), P(), P(), columns)
    return jax.shard_map(
        shards, mesh=mesh, in_specs=in_specs, out_specs=P("fsdp", "ctx", None), check_vma=False
    )
```

time: 1770 us -> 137 us (0.08)
  waiting for transfers between devices: 1400 us -> 0 us
  Pallas kernels: 0 us -> 135 us
  local copies, waits for them, and re-layouts: 128 us -> 2.3 us
  other arithmetic: 107 us -> 0 us
  blocking collectives: 79.9 us -> 0 us
  matrix products: 28.6 us -> 0 us
    all_gather x5 -> x0, waiting for transfers between devices: 1400 us -> none  [the longest x1 426 us: shards(): lax.all_gather(zx_weight, ('fsdp', 'ctx'), axis=1, tiled=True)]
    pallas_call x0 -> x1, Pallas kernels: none -> 135 us  [layer(): pl.pallas_call(kernel, out_shape=jax.ShapeDtypeStruct((256, 2048), BF16),...]
    select_n x63 -> x0, other arithmetic: 91 us -> none  [the longest x62 91 us: hop(): jnp.where(position < mine, new, old)]
    all_gather x2 -> x0, blocking collectives: 79.9 us -> none  [entering_2(): pieces = jax.tree.map(lambda part: lax.all_gather(part, axis), value)]
    rev x8 -> x0, local copies, waits for them, and re-layouts: 48.7 us -> none  [the longest x2 24.3 us: entering_2(): pieces = jax.tree.map(lambda part: part[::-1], pieces)]
    mul x65 -> x0, local copies, waits for them, and re-layouts: 43.6 us -> none  [the longest x62 42.8 us: chain(): later[0][:, None, None] * earlier[1] + later[1]]
    dot_general x12 -> x0, matrix products: 28.6 us -> none  [the longest x2 9.16 us: project(): jnp.dot(token_rows, piece, preferred_element_type=jnp.float32)]
    reshape x10 -> x0, local copies, waits for them, and re-layouts: 19.1 us -> none  [the longest x4 16.2 us: finish(): summed.reshape(summed.shape[0] * summed.shape[1], summed.shape[2] * summe...]
  transfers between devices with their start and end apart: 5 -> 0, of which waited for: 5 -> 0; matrix products, arithmetic and copies ran while one was open for 13% -> 0% of each run, Pallas kernels for 0% -> 0%
where the time goes in v2:
time: 137 us
  Pallas kernels  135 us (99%)
  local copies, waits for them, and re-layouts  2.3 us (2%)
    pallas_call x1, Pallas kernels, layer(): pl.pallas_call(kernel, out_shape=jax.ShapeDtypeStruct((256, 2048), BF16),...  135 us

profile of v2, /device:TPU:1, one launch (start us, length us, event | category | flops | bytes accessed | tf_op | source)
XLA Modules:
  0.0 137.2 jit_solution(16245534908321202640)
XLA Ops:
  0.0 134.9 %layer.1 = bf16[256,2048]{1,0:T(8,128)(2,1)} custom-call(bf16[16,2048]{1,0:T(8,128)(2,1)} %bitcast.18, bf16[2,2048]{1,0:T(2,128)(2,1)} %bitcast.20, bf16[16,1024]{1,0:T(8,128)(2,1)} %bitcast.19, bf16[256,2048]{1,0:T(8,128)(2,1)} %bitcast.16, bf16[64,2048]{1,0:T(8,128)(2,1)} %bitcast.17, f32[1,32]{1,0:T(1,128)} %bitcast.22, f32[1,32]{1,0:T(1,128)} %bitcast.23, ...), custom_call_target="tpu_custom_call" | custom-call | tf_op jit(solution)/shard_map/layer/pallas_call | solution.py:514
  134.9 2.3 %copy.10 = bf16[1,256,2048]{2,1,0:T(8,128)(2,1)} copy(bf16[1,256,2048]{2,1,0:T(8,128)(2,1)} %bitcast.15) | data formatting | bytes 2097152

commit v3 on v2

--- a/solution.py
+++ b/solution.py
@@ -149,8 +149,8 @@
     wz, wb, wo, xs, bst, bstf, bcs, ows, bcm, bcf, owm, owf,
     inner, bco, lams, dts, lamt, wide_f, wide_l, wm, kst, dend, yo, enter,
     pay, got, reply, ent, gbuf, wide, sqb, sqf,
-    zsend, zrecv, bsend, brecv, osend, orecv, local,
-    gs, gr, swap_s, swap_r, s1, r1, s2, r2, ps, pr,
+    d0s, d0r, zs_s, zs_r, local, gs, gr, ozs, ozr, osw_s, osw_r,
+    swap_s, swap_r, s1, r1, s2, r2, ps, pr,
 ):
     y, xl, z, xh, core = coords()
     x = xh * 2 + xl
@@ -171,16 +171,15 @@
         )
 
     barrier = pltpu.get_barrier_semaphore()
-    peers = []
-    for dz in range(8):
-        for dc in range(2):
-            for dy in (0, 2):
-                if (dz, dc, dy) != (0, 0, 0):
-                    peers.append(dev((y + dy) % 4, x, (z + dz) % 8, (core + dc) % 2))
-        peers.append(dev(y, (x + 2) % 4, (z + dz) % 8, core))
+    peers = [partner, dev((y + 2) % 4, x, z, core), dev((y + 2) % 4, x, z, 1 - core)]
     for k in (1, 3):
         peers.append(dev((y + k) % 4, x, z, core))
         peers.append(dev(y, (x + k) % 4, z, core))
+    for k in (1, 7):
+        peers.append(dev(y, x, (z + k) % 8, core))
+    for k in range(1, 16):
+        if k not in (2, 14):
+            peers.append(state_peer((chip + k) % 16))
     for to in peers:
         pl.semaphore_signal(barrier, inc=1, device_id=to, device_id_type=MESH)
     for j in range(8):
@@ -188,46 +187,81 @@
     bst[...] = bstf[...].astype(BF16)
     pl.semaphore_wait(barrier, len(peers))
 
-    def first(src, dst, to_y, send, recv):
-        is_self = jnp.logical_and(to_y == y, h == core)
-        for dz in (0, 1, 7, 2, 6, 3, 5, 4):
-            c = remote(src, dst, send.at[dz], recv, dev(to_y, x, (z + dz) % 8, h))
-            if dz:
-                c.start()
-            else:
-
-                @pl.when(is_self)
-                def _():
-                    pltpu.make_async_copy(src, dst, recv).start()
-
-                @pl.when(jnp.logical_not(is_self))
-                def _():
-                    c.start()
-
-        def done():
-            for dz in range(8):
-                if dz:
-                    wait_bytes(src, send.at[dz])
-                else:
-
-                    @pl.when(jnp.logical_not(is_self))
-                    def _():
-                        wait_bytes(src, send.at[0])
-
-        return done
-
     def own_z(g, sy, sl, src_core):
         return wz.at[g, sy, xl, sl, xh, pl.ds(src_core * 16, 16)]
 
+    def home(src, dst, to_y, kind):
+        is_self = jnp.logical_and(to_y == y, h == core)
+        far = remote(src, dst, d0s.at[kind], d0r.at[kind, core], dev(to_y, x, z, h))
+
+        @pl.when(is_self)
+        def _():
+            pltpu.make_async_copy(src, dst, d0r.at[kind, core]).start()
+
+        @pl.when(jnp.logical_not(is_self))
+        def _():
+            far.start()
+
+        def done():
+            @pl.when(jnp.logical_not(is_self))
+            def _():
+                far.wait_send()
+
+        return done
+
     dones = [
-        first(bst, bcs.at[zc, core], y, bsend, brecv.at[zc, core]),
-        first(zx, own_z(inner_side, ys, zl, core), y_to, zsend, zrecv.at[inner_side, zl, core]),
+        home(bst, bcs.at[zc, core], y, 0),
+        home(zx, own_z(inner_side, ys, zl, core), y_to, 1),
     ]
+    merge = remote(ow, ows.at[core], swap_s.at[2], swap_r.at[2], partner)
+    merge.start()
+    merge_own = pltpu.make_async_copy(ow, ows.at[core], local.at[2])
+    merge_own.start()
     tok_own = pltpu.make_async_copy(tok, xs.at[core], local.at[0])
     tok_own.start()
     tok_far = remote(tok, xs.at[core], swap_s.at[0], swap_r.at[0], partner)
     tok_far.start()
-    dones.append(first(ow, ows.at[zc, core], y, osend, orecv.at[zc, core]))
+
+    def kept(zsrc):
+        q = zsrc % 4
+        side = 1 - (q // 2 + y // 2) % 2
+        return q, bcs.at[q], wz.at[side, yy + 2 * (q // 2), xl, q % 2, xh]
+
+    def hop(zsrc, d, way):
+        q, b_ref, z_ref = kept(zsrc)
+        mine_now = zsrc // 4 == core
+        ways = (0, 1) if d == 0 else (way,) if d < (4 if way == 0 else 3) else ()
+        out = []
+        for w in ways:
+            to = dev(y, x, (z + 1 + 6 * w) % 8, core)
+            out.append(remote(b_ref, b_ref, zs_s.at[0, w, d], zs_r.at[0, q], to))
+            out.append(remote(z_ref, z_ref, zs_s.at[1, w, d], zs_r.at[1, q], to))
+
+        @pl.when(mine_now)
+        def _():
+            if d == 0:
+                for s in range(2):
+                    wait_bytes(bcs.at[q, s], d0r.at[0, s])
+                for s in range(2):
+                    wait_bytes(z_ref.at[pl.ds(16 * s, 16)], d0r.at[1, s])
+            else:
+                wait_bytes(b_ref, zs_r.at[0, q])
+                wait_bytes(z_ref, zs_r.at[1, q])
+            for cp in out:
+                cp.start()
+
+        def done():
+            @pl.when(mine_now)
+            def _():
+                for cp in out:
+                    cp.wait_send()
+
+        dones.append(done)
+
+    def hops(d):
+        hop((z - d) % 8, d, 0)
+        if 0 < d < 4:
+            hop((z + d) % 8, d, 1)
 
     def view_b(half, sy, sx, part):
         lanes = pl.ds(1024 * half, 1024) if part is None else pl.ds(1024 * half + 512 * part, 512)
@@ -240,9 +274,43 @@
 
         return view
 
+    my_lanes = pl.multiple_of(1024 * core, 1024)
+
     def view_o(half, sy, sx, part):
-        tiles = pl.ds(2 * half, 2) if part is None else pl.ds(2 * half + part, 1)
-        return wo.at[sy, sx % 2, core, tiles, sx // 2]
+        lanes = pl.ds(my_lanes + 512 * half, 512) if part is None else pl.ds(my_lanes + 512 * half + 256 * part, 256)
+        return wo.at[sy, sx % 2, z, sx // 2, :, lanes]
+
+    def plane(zsrc, part):
+        return wo.at[:, :, zsrc, :, :, pl.ds(my_lanes + 512 * part, 512)]
+
+    o_copies = []
+
+    def o_send(zsrc, way, d, part):
+        ref = plane(zsrc, part)
+        to = dev(y, x, (z + 1 + 6 * way) % 8, core)
+        cp = remote(ref, ref, ozs.at[way, d, part], ozr.at[way, d, part], to)
+        cp.start()
+        o_copies.append(cp)
+
+    def o_swap(zsrc, index):
+        for part in range(2):
+            ref = plane(zsrc, part)
+            cp = remote(ref, ref, osw_s.at[index, part], osw_r.at[index, part], partner)
+            cp.start()
+            o_copies.append(cp)
+
+    def o_turn(d):
+        for way in range(2):
+            zsrc = (z - d) % 8 if way == 0 else (z + d) % 8
+            for part in range(2):
+                if d < 4 or part == way:
+                    wait_bytes(plane(zsrc, part), ozr.at[way, d - 1, part])
+                if d < 3 or (d == 3 and part == way):
+                    o_send(zsrc, way, d, part)
+        for way in range(2):
+            zsrc = (z - d) % 8 if way == 0 else (z + d) % 8
+            if d < 4 or way == 0:
+                o_swap(zsrc, d if way == 0 else 8 - d)
 
     same = lambda v: v
     flip = lambda v: (v + 2) % 4
@@ -251,9 +319,24 @@
     set_g = Ring(view_g(0), flip, gs.at[2], gr.at[2])
     set_o = Ring(view_o, same, gs.at[3], gr.at[3])
 
-    for q in range(4):
-        for s in range(2):
-            wait_bytes(bcs.at[q, s], brecv.at[q, s])
+    hops(0)
+    merge_own.wait()
+    wait_bytes(ows.at[1 - core], swap_r.at[2])
+    for s in range(2):
+        v = ows[s].astype(F32)
+        for j in range(2):
+            owf[8 * s : 8 * s + 8, 1024 * j : 1024 * j + 1024] = v[8 * j : 8 * j + 8, :]
+    owm[...] = owf[...].astype(BF16)
+    own_lanes = pl.ds(my_lanes, 1024)
+    put = pltpu.make_async_copy(owm.at[:, own_lanes], wo.at[y, xl, z, xh, :, own_lanes], local.at[2])
+    put.start()
+    hops(1)
+    put.wait()
+    set_o.begin()
+    hops(2)
+    hops(3)
+    hops(4)
+
     for q in range(4):
         for s in range(2):
             v = bcs[q, s].astype(F32)
@@ -264,12 +347,13 @@
     put.start()
     put.wait()
     set_b.begin()
-    for s in range(2):
-        for r in range(2):
-            wait_bytes(own_z(1, y, s, r), zrecv.at[1, s, r])
     set_i.begin()
+    set_o.first()
     set_b.first()
     set_i.first()
+    set_o.second()
+    for j in (0, 1, 3, 2):
+        set_o.third(j)
     set_b.second()
     set_i.second()
 
@@ -285,6 +369,12 @@
 
     set_b.third(0)
     set_i.third(0)
+    for j in range(4):
+        set_o.fourth(j)
+    for part in range(2):
+        for way in range(2):
+            o_send(z, way, 0, part)
+    o_swap(z, 0)
 
     def choose(ref):
         one = (lax.broadcasted_iota(jnp.int32, (32, 16), 0) == head_map(core, (32, 16), 1)).astype(BF16)
@@ -315,6 +405,7 @@
     set_i.third(3)
     set_b.third(2)
     set_i.third(2)
+    set_g.begin()
     for j in range(4):
         set_b.fourth(j)
     swaps = [remote(wb.at[:, core], wb.at[:, core], swap_s.at[1], swap_r.at[1], partner)]
@@ -352,24 +443,7 @@
 
     for j in range(4):
         set_i.fourth(j)
-    for q in range(4):
-        for s in range(2):
-            wait_bytes(ows.at[q, s], orecv.at[q, s])
-    for q in range(4):
-        for s in range(2):
-            v = ows[q, s].astype(F32)
-            for j in range(2):
-                owf[q, 8 * s : 8 * s + 8, 1024 * j : 1024 * j + 1024] = v[8 * j : 8 * j + 8, :]
-    owm[...] = owf[...].astype(BF16)
-    put = pltpu.make_async_copy(owm, wo.at[y, xl, core, :, xh], local.at[2])
-    put.start()
-    for s in range(2):
-        for q in range(2):
-            wait_bytes(own_z(0, flip(y), s, q), zrecv.at[0, s, q])
-    set_g.begin()
-    put.wait()
-    set_o.begin()
-
+    o_turn(1)
     for g in range(4):
         w = wz[1, g].reshape(256, 2048)
         inner[:, 256 * g : 256 * g + 256] = dot_nt(xs[...].reshape(ROWS, 2048), w).astype(BF16)
@@ -411,7 +485,7 @@
 
     state_copies = send_states(pay, got, s1, r1)
     set_g.first()
-    set_o.first()
+    set_g.second()
 
     left = lax.broadcasted_iota(jnp.int32, (BLOCK, BLOCK), 1) < 64
 
@@ -427,8 +501,9 @@
 
     lax.fori_loop(0, NBLK, block_intra, 0)
 
-    set_g.second()
-    set_o.second()
+    o_turn(2)
+    for j in (0, 1, 3, 2):
+        set_g.third(j)
     wait_states(got, r1)
     for d in range(2):
         state = jnp.zeros((64, 128), F32)
@@ -439,9 +514,14 @@
             state = de * state + got[i, 64 * d : 64 * d + 64, :].astype(F32)
     state_copies += send_states(reply, ent, s2, r2)
 
-    for j in (0, 1, 3, 2):
-        set_g.third(j)
-        set_o.third(j)
+    o_turn(3)
+    for j in range(4):
+        set_g.fourth(j)
+    for g in range(4):
+        w = wz[0, g].reshape(256, 2048)
+        gate = dot_nt(xs[...].reshape(ROWS, 2048), w).astype(BF16).astype(F32)
+        wide_f[0, :, 256 * g : 256 * g + 256] = gate / (1.0 + jnp.exp(-gate))
+    o_turn(4)
     wait_states(ent, r2)
     for q in range(8):
         cols = slice(128 * q, 128 * q + 128)
@@ -457,16 +537,13 @@
             yo[rows, :] = yo[rows, :] + wide_l[d, rows, :] * dot_nn(cv, state.astype(BF16))
             state = dend[d, b] * state + kst[d, b]
 
-    for j in range(4):
-        set_g.fourth(j)
     theirs = pl.ds(pl.multiple_of((1 - core) * 256, 256), 256)
     mine = pl.ds(pl.multiple_of(core * 256, 256), 256)
     squares = jnp.zeros((ROWS, 1), F32)
     pair_copies = []
     for g in range(4):
-        w = wz[0, g].reshape(256, 2048)
-        gate = dot_nt(xs[...].reshape(ROWS, 2048), w).astype(BF16).astype(F32)
-        gated = yo[:, 256 * g : 256 * g + 256] * (gate / (1.0 + jnp.exp(-gate)))
+        cols = slice(256 * g, 256 * g + 256)
+        gated = yo[:, cols] * wide_f[0, :, cols]
         squares = squares + jnp.sum(gated * gated, axis=1, keepdims=True)
         for i in range(2 * g, 2 * g + 2):
             place = pl.ds(natural(core, i), 128)
@@ -482,15 +559,14 @@
     cp.start()
     pair_copies.append(cp)
 
-    for j in range(4):
-        set_o.fourth(j)
-    swaps.append(remote(wo.at[:, :, core], wo.at[:, :, core], swap_s.at[2], swap_r.at[2], partner))
-    swaps[1].start()
     for i in range(8):
         wait_bytes(wide.at[:, pl.ds(natural(1 - core, i), 128)], pr.at[i])
     wait_bytes(sqf, pr.at[8])
     scale = lax.rsqrt((sqb[mine, :1] + sqf[:, :1]) * (1.0 / 2048.0) + 1e-05)
-    wait_bytes(wo.at[:, :, 1 - core], swap_r.at[2])
+    far_lanes = pl.multiple_of(1024 * (1 - core), 1024)
+    for d in range(8):
+        for part in range(2):
+            wait_bytes(wo.at[:, :, (z - d) % 8, :, :, pl.ds(far_lanes + 512 * part, 512)], osw_r.at[d, part])
     for g in range(8):
         w = wo[g // 2, g % 2].reshape(256, 2048)
         result[:, 256 * g : 256 * g + 256] = (dot_nt(wide[...], w) * scale).astype(BF16)
@@ -500,7 +576,8 @@
     for s in (set_b, set_i, set_g, set_o):
         s.drain()
     tok_far.wait_send()
-    for cp in swaps + state_copies + pair_copies:
+    merge.wait_send()
+    for cp in swaps + state_copies + pair_copies + o_copies:
         cp.wait_send()
 
 
@@ -518,10 +595,10 @@
         out_specs=INV,
         scratch_shapes=[
             vm((2, 4, 2, 2, 2, 32, 2048), BF16), vm((4, 2, 2, 2, 16, 2048), BF16),
-            vm((4, 2, 2, 4, 2, 16, 2048), BF16), vm((2, 256, 2048), BF16),
+            vm((4, 2, 8, 2, 16, 2048), BF16), vm((2, 256, 2048), BF16),
             vm((16, 256), BF16), vm((16, 256), F32),
-            vm((4, 2, 16, 256), BF16), vm((4, 2, 16, 1024), BF16),
-            vm((16, 2048), BF16), vm((16, 2048), F32), vm((4, 16, 2048), BF16), vm((4, 16, 2048), F32),
+            vm((4, 2, 16, 256), BF16), vm((2, 16, 1024), BF16),
+            vm((16, 2048), BF16), vm((16, 2048), F32), vm((16, 2048), BF16), vm((16, 2048), F32),
             vm((ROWS, WIDE), BF16), vm((ROWS, 512), BF16), vm((ROWS, 32), F32), vm((ROWS, 32), F32),
             vm((NBLK, 32, BLOCK), F32), vm((2, ROWS, WIDE), F32), vm((2, ROWS, WIDE), F32),
             vm((NBLK, BLOCK, 2048), BF16), vm((2, NBLK, BLOCK, WIDE), F32), vm((2, NBLK, 1, WIDE), F32),
@@ -529,8 +606,8 @@
             vm((16, 144, 128), BF16), vm((16, 144, 128), BF16), vm((16, 128, 128), BF16),
             vm((16, 128, 128), BF16), vm((ROWS, WIDE), BF16), vm((256, 2048), BF16),
             vm((ROWS, 128), F32), vm((256, 128), F32),
-            dma((8,)), dma((2, 2, 2)), dma((8,)), dma((4, 2)), dma((8,)), dma((4, 2)), dma((3,)),
-            dma((4, 2, 20)), dma((4, 2, 20)), dma((3,)), dma((3,)),
+            dma((2,)), dma((2, 2)), dma((2, 2, 4)), dma((2, 4)), dma((3,)), dma((4, 2, 20)), dma((4, 2, 20)),
+            dma((2, 4, 2)), dma((2, 4, 2)), dma((8, 2)), dma((8, 2)), dma((3,)), dma((3,)),
             dma((15,)), dma((15,)), dma((15,)), dma((15,)), dma((9,)), dma((9,)),
         ],
         compiler_params=pltpu.CompilerParams(

time: 137 us -> 136 us (level)
  Pallas kernels: 135 us -> 133 us
    pallas_call x1, Pallas kernels: 135 us -> 133 us  [layer(): pl.pallas_call(kernel, out_shape=jax.ShapeDtypeStruct((256, 2048), BF16),...]
where the time goes in v3:
time: 136 us; the launch traced here: 135 us
  Pallas kernels  133 us (98%)
  local copies, waits for them, and re-layouts  2.3 us (2%)
    pallas_call x1, Pallas kernels, layer(): pl.pallas_call(kernel, out_shape=jax.ShapeDtypeStruct((256, 2048), BF16),...  133 us

profile of v3, /device:TPU:1, one launch (start us, length us, event | category | flops | bytes accessed | tf_op | source)
XLA Modules:
  0.0 135.2 jit_solution(17783199672707583947)
XLA Ops:
  0.0 132.8 %layer.1 = bf16[256,2048]{1,0:T(8,128)(2,1)} custom-call(bf16[16,2048]{1,0:T(8,128)(2,1)} %bitcast.18, bf16[2,2048]{1,0:T(2,128)(2,1)} %bitcast.20, bf16[16,1024]{1,0:T(8,128)(2,1)} %bitcast.19, bf16[256,2048]{1,0:T(8,128)(2,1)} %bitcast.16, bf16[64,2048]{1,0:T(8,128)(2,1)} %bitcast.17, f32[1,32]{1,0:T(1,128)} %bitcast.22, f32[1,32]{1,0:T(1,128)} %bitcast.23, ...), custom_call_target="tpu_custom_call" | custom-call | tf_op jit(solution)/shard_map/layer/pallas_call | solution.py:591
  132.8 2.3 %copy.10 = bf16[1,256,2048]{2,1,0:T(8,128)(2,1)} copy(bf16[1,256,2048]{2,1,0:T(8,128)(2,1)} %bitcast.15) | data formatting | bytes 2097152

commit v4 on v2

--- a/solution.py
+++ b/solution.py
@@ -148,9 +148,9 @@
     zx, bc, ow, tok, dtw, decay, skip, gain, result,
     wz, wb, wo, xs, bst, bstf, bcs, ows, bcm, bcf, owm, owf,
     inner, bco, lams, dts, lamt, wide_f, wide_l, wm, kst, dend, yo, enter,
-    pay, got, reply, ent, gbuf, wide, sqb, sqf,
-    zsend, zrecv, bsend, brecv, osend, orecv, local,
-    gs, gr, swap_s, swap_r, s1, r1, s2, r2, ps, pr,
+    pay_f, pay_b, got_f, got_b, reply, ent, gbuf, wide, sqb, sqf,
+    zsend, zrecv, bsend, brecv, local, gs, gr, ozs, ozr, osw_s, osw_r, o2s, o2r,
+    swap_s, swap_r, s1, r1, s2, r2, ps, pr,
 ):
     y, xl, z, xh, core = coords()
     x = xh * 2 + xl
@@ -188,6 +188,9 @@
     bst[...] = bstf[...].astype(BF16)
     pl.semaphore_wait(barrier, len(peers))
 
+    def own_z(g, sy, sl, src_core):
+        return wz.at[g, sy, xl, sl, xh, pl.ds(src_core * 16, 16)]
+
     def first(src, dst, to_y, send, recv):
         is_self = jnp.logical_and(to_y == y, h == core)
         for dz in (0, 1, 7, 2, 6, 3, 5, 4):
@@ -216,18 +219,18 @@
 
         return done
 
-    def own_z(g, sy, sl, src_core):
-        return wz.at[g, sy, xl, sl, xh, pl.ds(src_core * 16, 16)]
-
     dones = [
         first(bst, bcs.at[zc, core], y, bsend, brecv.at[zc, core]),
         first(zx, own_z(inner_side, ys, zl, core), y_to, zsend, zrecv.at[inner_side, zl, core]),
     ]
+    merge = remote(ow, ows.at[core], swap_s.at[2], swap_r.at[2], partner)
+    merge.start()
+    merge_own = pltpu.make_async_copy(ow, ows.at[core], local.at[2])
+    merge_own.start()
     tok_own = pltpu.make_async_copy(tok, xs.at[core], local.at[0])
     tok_own.start()
     tok_far = remote(tok, xs.at[core], swap_s.at[0], swap_r.at[0], partner)
     tok_far.start()
-    dones.append(first(ow, ows.at[zc, core], y, osend, orecv.at[zc, core]))
 
     def view_b(half, sy, sx, part):
         lanes = pl.ds(1024 * half, 1024) if part is None else pl.ds(1024 * half + 512 * part, 512)
@@ -240,38 +243,80 @@
 
         return view
 
-    def view_o(half, sy, sx, part):
-        tiles = pl.ds(2 * half, 2) if part is None else pl.ds(2 * half + part, 1)
-        return wo.at[sy, sx % 2, core, tiles, sx // 2]
+    my_lanes = pl.multiple_of(1024 * core, 1024)
+
+    my_lanes = pl.multiple_of(1024 * core, 1024)
+    far_lanes = pl.multiple_of(1024 * (1 - core), 1024)
+
+    def view_o1(half, sy, sx, part):
+        lanes = pl.ds(my_lanes + 256 * half, 256) if part is None else pl.ds(my_lanes + 256 * half + 128 * part, 128)
+        return wo.at[sy, sx % 2, z, sx // 2, :, lanes]
+
+    def view_o2(half, sy, sx, part):
+        zs = pl.ds(4 * half, 4) if part is None else pl.ds(4 * half + 2 * part, 2)
+        return wo.at[sy, sx % 2, zs, sx // 2, :, pl.ds(my_lanes + 512, 512)]
+
+    def plane(zsrc, part, base=None):
+        return wo.at[:, :, zsrc, :, :, pl.ds((my_lanes if base is None else base) + 256 * part, 256)]
+
+    def corner(half, j, base):
+        lanes = pl.ds(base + 512, 512)
+        if half == 0:
+            return wo.at[(y - j) % 4, :, pl.ds(0, 4), :, :, lanes]
+        sx = (x - j) % 4
+        return wo.at[:, sx % 2, pl.ds(4, 4), sx // 2, :, lanes]
+
+    o_copies = []
+
+    def o_send(zsrc, way, d, part):
+        ref = plane(zsrc, part)
+        to = dev(y, x, (z + 1 + 6 * way) % 8, core)
+        cp = remote(ref, ref, ozs.at[way, d, part], ozr.at[way, d, part], to)
+        cp.start()
+        o_copies.append(cp)
+
+    def o_hand(ref, index):
+        cp = remote(ref, ref, osw_s.at[index], osw_r.at[index], partner)
+        cp.start()
+        o_copies.append(cp)
+
+    def o_swap(zsrc, d):
+        for part in range(2):
+            o_hand(plane(zsrc, part), 2 * d + part)
+
+    def o_turn(d):
+        for way in range(2):
+            zsrc = (z - d) % 8 if way == 0 else (z + d) % 8
+            for part in range(2):
+                if d < 4 or part == way:
+                    wait_bytes(plane(zsrc, part), ozr.at[way, d - 1, part])
+                if d < 3 or (d == 3 and part == way):
+                    o_send(zsrc, way, d, part)
+        for way in range(2):
+            zsrc = (z - d) % 8 if way == 0 else (z + d) % 8
+            if d < 4 or way == 0:
+                o_swap(zsrc, d if way == 0 else 8 - d)
 
     same = lambda v: v
     flip = lambda v: (v + 2) % 4
     set_b = Ring(view_b, same, gs.at[0], gr.at[0])
     set_i = Ring(view_g(1), same, gs.at[1], gr.at[1])
     set_g = Ring(view_g(0), flip, gs.at[2], gr.at[2])
-    set_o = Ring(view_o, same, gs.at[3], gr.at[3])
-
-    for q in range(4):
-        for s in range(2):
-            wait_bytes(bcs.at[q, s], brecv.at[q, s])
-    for q in range(4):
-        for s in range(2):
-            v = bcs[q, s].astype(F32)
-            for j in range(8):
-                bcf[4 * q + 2 * s : 4 * q + 2 * s + 2, 256 * j : 256 * j + 256] = v[2 * j : 2 * j + 2, :]
-    bcm[...] = bcf[...].astype(BF16)
-    put = pltpu.make_async_copy(bcm, wb.at[y, core, xl, xh], local.at[1])
+    set_o = Ring(view_o1, same, gs.at[3], gr.at[3])
+    set_p = Ring(view_o2, same, gs.at[4], gr.at[4])
+
+    merge_own.wait()
+    wait_bytes(ows.at[1 - core], swap_r.at[2])
+    for s in range(2):
+        v = ows[s].astype(F32)
+        for j in range(2):
+            owf[8 * s : 8 * s + 8, 1024 * j : 1024 * j + 1024] = v[8 * j : 8 * j + 8, :]
+    owm[...] = owf[...].astype(BF16)
+    own_lanes = pl.ds(my_lanes, 1024)
+    put = pltpu.make_async_copy(owm.at[:, own_lanes], wo.at[y, xl, z, xh, :, own_lanes], local.at[2])
     put.start()
     put.wait()
-    set_b.begin()
-    for s in range(2):
-        for r in range(2):
-            wait_bytes(own_z(1, y, s, r), zrecv.at[1, s, r])
-    set_i.begin()
-    set_b.first()
-    set_i.first()
-    set_b.second()
-    set_i.second()
+    set_o.begin()
 
     tok_own.wait()
     wait_bytes(xs.at[1 - core], swap_r.at[0])
@@ -282,9 +327,6 @@
     v = dot_nn(raw, pick.astype(BF16))
     dt = jnp.maximum(v, 0.0) + jnp.log1p(jnp.exp(-jnp.abs(v)))
     dts[...] = dt
-
-    set_b.third(0)
-    set_i.third(0)
 
     def choose(ref):
         one = (lax.broadcasted_iota(jnp.int32, (32, 16), 0) == head_map(core, (32, 16), 1)).astype(BF16)
@@ -309,17 +351,6 @@
         padded = jnp.concatenate([lam - logdt[rows], jnp.zeros((BLOCK, 96), F32)], axis=1)
         lamt[b] = jnp.transpose(padded)[:32]
 
-    set_b.third(1)
-    set_b.third(3)
-    set_i.third(1)
-    set_i.third(3)
-    set_b.third(2)
-    set_i.third(2)
-    for j in range(4):
-        set_b.fourth(j)
-    swaps = [remote(wb.at[:, core], wb.at[:, core], swap_s.at[1], swap_r.at[1], partner)]
-    swaps[0].start()
-
     for d in range(2):
         cols = slice(16 * d, 16 * d + 16)
         for b in range(NBLK):
@@ -331,6 +362,54 @@
             wide_l[d, rows, :] = wl
             dend[d, b] = wl[BLOCK - 1 : BLOCK] if d == 0 else wl[0:1]
 
+
+    set_o.first()
+    set_o.second()
+    for j in (0, 1, 3, 2):
+        set_o.third(j)
+
+    for q in range(4):
+        for s in range(2):
+            wait_bytes(bcs.at[q, s], brecv.at[q, s])
+    for q in range(4):
+        for s in range(2):
+            v = bcs[q, s].astype(F32)
+            for j in range(8):
+                bcf[4 * q + 2 * s : 4 * q + 2 * s + 2, 256 * j : 256 * j + 256] = v[2 * j : 2 * j + 2, :]
+    bcm[...] = bcf[...].astype(BF16)
+    put = pltpu.make_async_copy(bcm, wb.at[y, core, xl, xh], local.at[1])
+    put.start()
+    put.wait()
+    set_b.begin()
+    for s in range(2):
+        for q in range(2):
+            wait_bytes(own_z(1, y, s, q), zrecv.at[1, s, q])
+    set_i.begin()
+    for j in range(4):
+        set_o.fourth(j)
+    for part in range(2):
+        for way in range(2):
+            o_send(z, way, 0, part)
+    o_swap(z, 0)
+    set_b.first()
+    set_i.first()
+    for k in (1, 7, 2, 6, 3, 5, 4):
+        ref = wo.at[y, xl, z, xh, :, pl.ds(my_lanes + 512, 512)]
+        cp = remote(ref, ref, o2s.at[k - 1], o2r.at[k - 1], dev(y, x, (z + k) % 8, core))
+        cp.start()
+        o_copies.append(cp)
+    set_b.second()
+    set_i.second()
+    for j in (0, 1, 3, 2):
+        set_b.third(j)
+        set_i.third(j)
+        if j == 1:
+            o_turn(1)
+    for j in range(4):
+        set_b.fourth(j)
+    swaps = [remote(wb.at[:, core], wb.at[:, core], swap_s.at[1], swap_r.at[1], partner)]
+    swaps[0].start()
+    o_turn(2)
     wait_bytes(wb.at[:, 1 - core], swap_r.at[1])
     bco[...] = dot_nt(xs[...].reshape(ROWS, 2048), wb[...].reshape(512, 2048)).astype(BF16)
 
@@ -352,52 +431,20 @@
 
     for j in range(4):
         set_i.fourth(j)
-    for q in range(4):
-        for s in range(2):
-            wait_bytes(ows.at[q, s], orecv.at[q, s])
-    for q in range(4):
-        for s in range(2):
-            v = ows[q, s].astype(F32)
-            for j in range(2):
-                owf[q, 8 * s : 8 * s + 8, 1024 * j : 1024 * j + 1024] = v[8 * j : 8 * j + 8, :]
-    owm[...] = owf[...].astype(BF16)
-    put = pltpu.make_async_copy(owm, wo.at[y, xl, core, :, xh], local.at[2])
-    put.start()
     for s in range(2):
         for q in range(2):
             wait_bytes(own_z(0, flip(y), s, q), zrecv.at[0, s, q])
     set_g.begin()
-    put.wait()
-    set_o.begin()
-
+    for k in range(1, 8):
+        wait_bytes(wo.at[y, xl, (z - k) % 8, xh, :, pl.ds(my_lanes + 512, 512)], o2r.at[k - 1])
+    set_p.begin()
     for g in range(4):
         w = wz[1, g].reshape(256, 2048)
         inner[:, 256 * g : 256 * g + 256] = dot_nt(xs[...].reshape(ROWS, 2048), w).astype(BF16)
 
-    decay_rows = []
-    for d in range(2):
-        state = jnp.zeros((BLOCK, WIDE), F32)
-        decays = jnp.ones((1, WIDE), F32)
-        for b in range(NBLK) if d == 0 else reversed(range(NBLK)):
-            rows = slice(b * BLOCK, b * BLOCK + BLOCK)
-            scaled = (wide_f[d, rows, :] * inner[rows, :].astype(F32)).astype(BF16)
-            k = dot_tn(bco[rows, 256 * d : 256 * d + 128], scaled)
-            de = dend[d, b]
-            kst[d, b] = k
-            state = de * state + k
-            decays = decays * de
-        for j in range(16):
-            q, nh = j // 2, j % 2
-            pay[j, 64 * d : 64 * d + 64, :] = state[64 * nh : 64 * nh + 64, 128 * q : 128 * q + 128].astype(BF16)
-        decay_rows += list(parts3(decays))
-    tail = jnp.concatenate([p.astype(F32) for p in decay_rows] + [jnp.zeros((10, WIDE), F32)], axis=0).astype(BF16)
-    for j in range(16):
-        q = j // 2
-        pay[j, 128:144, :] = tail[:, 128 * q : 128 * q + 128]
-
     def send_states(src, dst, ss, rs):
         cs = []
-        for k in range(1, 16):
+        for k in (8, 7, 9, 6, 10, 5, 11, 4, 12, 3, 13, 2, 14, 1, 15):
             j = (chip + k) % 16
             c = remote(src.at[j], dst.at[chip], ss.at[k - 1], rs.at[k - 1], state_peer(j))
             c.start()
@@ -409,9 +456,32 @@
         for k in range(1, 16):
             wait_bytes(dst.at[(chip - k) % 16], rs.at[k - 1])
 
-    state_copies = send_states(pay, got, s1, r1)
+    both_decays = []
+    for d in range(2):
+        decays = dend[d, 0]
+        for b in range(1, NBLK):
+            decays = decays * dend[d, b]
+        both_decays += [p.astype(F32) for p in parts3(decays)]
+    tail = jnp.concatenate(both_decays + [jnp.zeros((10, WIDE), F32)], axis=0).astype(BF16)
+    state_copies = []
+    for d in range(2):
+        pay = (pay_f, pay_b)[d]
+        state = jnp.zeros((BLOCK, WIDE), F32)
+        for b in range(NBLK) if d == 0 else reversed(range(NBLK)):
+            rows = slice(b * BLOCK, b * BLOCK + BLOCK)
+            scaled = (wide_f[d, rows, :] * inner[rows, :].astype(F32)).astype(BF16)
+            k = dot_tn(bco[rows, 256 * d : 256 * d + 128], scaled)
+            kst[d, b] = k
+            state = dend[d, b] * state + k
+        for j in range(16):
+            q, nh = j // 2, j % 2
+            pay[j, :64, :] = state[64 * nh : 64 * nh + 64, 128 * q : 128 * q + 128].astype(BF16)
+            if d == 0:
+                pay[j, 64:80, :] = tail[:, 128 * q : 128 * q + 128]
+        state_copies += send_states(pay, (got_f, got_b)[d], s1.at[d], r1.at[d])
+    o_turn(3)
     set_g.first()
-    set_o.first()
+    set_g.second()
 
     left = lax.broadcasted_iota(jnp.int32, (BLOCK, BLOCK), 1) < 64
 
@@ -427,46 +497,50 @@
 
     lax.fori_loop(0, NBLK, block_intra, 0)
 
-    set_g.second()
-    set_o.second()
-    wait_states(got, r1)
     for d in range(2):
+        got = (got_f, got_b)[d]
+        wait_states(got, r1.at[d])
         state = jnp.zeros((64, 128), F32)
         for i in range(16) if d == 0 else reversed(range(16)):
-            reply[i, 64 * d : 64 * d + 64, :] = state.astype(BF16)
-            ds = got[i, 128:144, :].astype(F32)
+            reply[d, i] = state.astype(BF16)
+            ds = got_f[i, 64:80, :].astype(F32)
             de = ds[3 * d : 3 * d + 1] + ds[3 * d + 1 : 3 * d + 2] + ds[3 * d + 2 : 3 * d + 3]
-            state = de * state + got[i, 64 * d : 64 * d + 64, :].astype(F32)
-    state_copies += send_states(reply, ent, s2, r2)
-
+            state = de * state + got[i, :64, :].astype(F32)
+        state_copies += send_states(reply.at[d], ent.at[d], s2.at[d], r2.at[d])
+        if d == 0:
+            set_p.first()
+            set_p.second()
     for j in (0, 1, 3, 2):
         set_g.third(j)
-        set_o.third(j)
-    wait_states(ent, r2)
-    for q in range(8):
-        cols = slice(128 * q, 128 * q + 128)
-        for nh in range(2):
-            piece = ent[2 * q + nh].astype(F32)
-            enter[0, 64 * nh : 64 * nh + 64, cols] = piece[:64]
-            enter[1, 64 * nh : 64 * nh + 64, cols] = piece[64:]
+    o_turn(4)
+    for j in (0, 1, 3, 2):
+        set_p.third(j)
+    for j in range(4):
+        set_g.fourth(j)
+    for g in range(4):
+        w = wz[0, g].reshape(256, 2048)
+        gate = dot_nt(xs[...].reshape(ROWS, 2048), w).astype(BF16).astype(F32)
+        wide_f[0, :, 256 * g : 256 * g + 256] = gate / (1.0 + jnp.exp(-gate))
     for d in range(2):
-        state = enter[d]
+        wait_states(ent.at[d], r2.at[d])
+        for q in range(8):
+            cols = slice(128 * q, 128 * q + 128)
+            for nh in range(2):
+                enter[64 * nh : 64 * nh + 64, cols] = ent[d, 2 * q + nh].astype(F32)
+        state = enter[...]
         for b in range(NBLK) if d == 0 else reversed(range(NBLK)):
             rows = slice(b * BLOCK, b * BLOCK + BLOCK)
             cv = bco[rows, 256 * d + 128 : 256 * d + 256]
             yo[rows, :] = yo[rows, :] + wide_l[d, rows, :] * dot_nn(cv, state.astype(BF16))
             state = dend[d, b] * state + kst[d, b]
 
-    for j in range(4):
-        set_g.fourth(j)
     theirs = pl.ds(pl.multiple_of((1 - core) * 256, 256), 256)
     mine = pl.ds(pl.multiple_of(core * 256, 256), 256)
     squares = jnp.zeros((ROWS, 1), F32)
     pair_copies = []
     for g in range(4):
-        w = wz[0, g].reshape(256, 2048)
-        gate = dot_nt(xs[...].reshape(ROWS, 2048), w).astype(BF16).astype(F32)
-        gated = yo[:, 256 * g : 256 * g + 256] * (gate / (1.0 + jnp.exp(-gate)))
+        cols = slice(256 * g, 256 * g + 256)
+        gated = yo[:, cols] * wide_f[0, :, cols]
         squares = squares + jnp.sum(gated * gated, axis=1, keepdims=True)
         for i in range(2 * g, 2 * g + 2):
             place = pl.ds(natural(core, i), 128)
@@ -482,25 +556,31 @@
     cp.start()
     pair_copies.append(cp)
 
-    for j in range(4):
-        set_o.fourth(j)
-    swaps.append(remote(wo.at[:, :, core], wo.at[:, :, core], swap_s.at[2], swap_r.at[2], partner))
-    swaps[1].start()
+    for j in (0, 1, 3, 2):
+        set_p.fourth(j)
+        for half in range(2):
+            o_hand(corner(half, j, my_lanes), 16 + 2 * j + half)
     for i in range(8):
         wait_bytes(wide.at[:, pl.ds(natural(1 - core, i), 128)], pr.at[i])
     wait_bytes(sqf, pr.at[8])
     scale = lax.rsqrt((sqb[mine, :1] + sqf[:, :1]) * (1.0 / 2048.0) + 1e-05)
-    wait_bytes(wo.at[:, :, 1 - core], swap_r.at[2])
+    for d in range(8):
+        for part in range(2):
+            wait_bytes(plane((z - d) % 8, part, far_lanes), osw_r.at[2 * d + part])
+    for j in range(4):
+        for half in range(2):
+            wait_bytes(corner(half, j, far_lanes), osw_r.at[16 + 2 * j + half])
     for g in range(8):
         w = wo[g // 2, g % 2].reshape(256, 2048)
         result[:, 256 * g : 256 * g + 256] = (dot_nt(wide[...], w) * scale).astype(BF16)
 
     for done in dones:
         done()
-    for s in (set_b, set_i, set_g, set_o):
+    for s in (set_b, set_i, set_g, set_o, set_p):
         s.drain()
     tok_far.wait_send()
-    for cp in swaps + state_copies + pair_copies:
+    merge.wait_send()
+    for cp in swaps + state_copies + pair_copies + o_copies:
         cp.wait_send()
 
 
@@ -518,20 +598,20 @@
         out_specs=INV,
         scratch_shapes=[
             vm((2, 4, 2, 2, 2, 32, 2048), BF16), vm((4, 2, 2, 2, 16, 2048), BF16),
-            vm((4, 2, 2, 4, 2, 16, 2048), BF16), vm((2, 256, 2048), BF16),
+            vm((4, 2, 8, 2, 16, 2048), BF16), vm((2, 256, 2048), BF16),
             vm((16, 256), BF16), vm((16, 256), F32),
-            vm((4, 2, 16, 256), BF16), vm((4, 2, 16, 1024), BF16),
-            vm((16, 2048), BF16), vm((16, 2048), F32), vm((4, 16, 2048), BF16), vm((4, 16, 2048), F32),
+            vm((4, 2, 16, 256), BF16), vm((2, 16, 1024), BF16),
+            vm((16, 2048), BF16), vm((16, 2048), F32), vm((16, 2048), BF16), vm((16, 2048), F32),
             vm((ROWS, WIDE), BF16), vm((ROWS, 512), BF16), vm((ROWS, 32), F32), vm((ROWS, 32), F32),
             vm((NBLK, 32, BLOCK), F32), vm((2, ROWS, WIDE), F32), vm((2, ROWS, WIDE), F32),
             vm((NBLK, BLOCK, 2048), BF16), vm((2, NBLK, BLOCK, WIDE), F32), vm((2, NBLK, 1, WIDE), F32),
-            vm((ROWS, WIDE), F32), vm((2, BLOCK, WIDE), F32),
-            vm((16, 144, 128), BF16), vm((16, 144, 128), BF16), vm((16, 128, 128), BF16),
-            vm((16, 128, 128), BF16), vm((ROWS, WIDE), BF16), vm((256, 2048), BF16),
+            vm((ROWS, WIDE), F32), vm((BLOCK, WIDE), F32),
+            vm((16, 80, 128), BF16), vm((16, 64, 128), BF16), vm((16, 80, 128), BF16), vm((16, 64, 128), BF16),
+            vm((2, 16, 64, 128), BF16), vm((2, 16, 64, 128), BF16), vm((ROWS, WIDE), BF16), vm((256, 2048), BF16),
             vm((ROWS, 128), F32), vm((256, 128), F32),
-            dma((8,)), dma((2, 2, 2)), dma((8,)), dma((4, 2)), dma((8,)), dma((4, 2)), dma((3,)),
-            dma((4, 2, 20)), dma((4, 2, 20)), dma((3,)), dma((3,)),
-            dma((15,)), dma((15,)), dma((15,)), dma((15,)), dma((9,)), dma((9,)),
+            dma((8,)), dma((2, 2, 2)), dma((8,)), dma((4, 2)), dma((3,)), dma((5, 2, 20)), dma((5, 2, 20)),
+            dma((2, 4, 2)), dma((2, 4, 2)), dma((24,)), dma((24,)), dma((7,)), dma((7,)), dma((3,)), dma((3,)),
+            dma((2, 15)), dma((2, 15)), dma((2, 15)), dma((2, 15)), dma((9,)), dma((9,)),
         ],
         compiler_params=pltpu.CompilerParams(
             collective_id=0, has_side_effects=True, vmem_limit_bytes=VMEM_BYTES

time: 137 us -> 124 us (0.905)
  Pallas kernels: 135 us -> 122 us
    pallas_call x1, Pallas kernels: 135 us -> 122 us  [layer(): pl.pallas_call(kernel, out_shape=jax.ShapeDtypeStruct((256, 2048), BF16),...]
where the time goes in v4:
time: 124 us
  Pallas kernels  122 us (98%)
  local copies, waits for them, and re-layouts  2.3 us (2%)
    pallas_call x1, Pallas kernels, layer(): pl.pallas_call(kernel, out_shape=jax.ShapeDtypeStruct((256, 2048), BF16),...  122 us

profile of v4, /device:TPU:1, one launch (start us, length us, event | category | flops | bytes accessed | tf_op | source)
XLA Modules:
  0.0 123.9 jit_solution(10189908397982738446)
XLA Ops:
  0.0 121.6 %layer.1 = bf16[256,2048]{1,0:T(8,128)(2,1)} custom-call(bf16[16,2048]{1,0:T(8,128)(2,1)} %bitcast.18, bf16[2,2048]{1,0:T(2,128)(2,1)} %bitcast.20, bf16[16,1024]{1,0:T(8,128)(2,1)} %bitcast.19, bf16[256,2048]{1,0:T(8,128)(2,1)} %bitcast.16, bf16[64,2048]{1,0:T(8,128)(2,1)} %bitcast.17, f32[1,32]{1,0:T(1,128)} %bitcast.22, f32[1,32]{1,0:T(1,128)} %bitcast.23, ...), custom_call_target="tpu_custom_call" | custom-call | tf_op jit(solution)/shard_map/layer/pallas_call | solution.py:594
  121.6 2.3 %copy.10 = bf16[1,256,2048]{2,1,0:T(8,128)(2,1)} copy(bf16[1,256,2048]{2,1,0:T(8,128)(2,1)} %bitcast.15) | data formatting | bytes 2097152

commit v5 on v4

--- a/solution.py
+++ b/solution.py
@@ -11,6 +11,7 @@
 F32 = jnp.float32
 BF16 = jnp.bfloat16
 BLOCK = 128
+PLANE_FIRST = 768
 ROWS = 512
 NBLK = ROWS // BLOCK
 WIDE = 1024
@@ -54,8 +55,8 @@
 
 
 class Ring:
-    def __init__(self, view, slot, send, recv):
-        self.view, self.slot, self.send, self.recv = view, slot, send, recv
+    def __init__(self, view, slot, send, recv, halves=(0, 1)):
+        self.view, self.slot, self.send, self.recv, self.halves = view, slot, send, recv, halves
         self.started = []
 
     def ref(self, half, j, m, part=None):
@@ -84,11 +85,11 @@
         self.copy(half, ref, 1, 3, 5 + 4 * j)
 
     def begin(self):
-        for half in range(2):
+        for half in self.halves:
             ref = self.ref(half, 0, 0)
             self.copy(half, ref, 0, 1, 0)
             self.copy(half, ref, 0, 3, 1)
-        for half in range(2):
+        for half in self.halves:
             self.both(half, 0)
 
     def turn(self, half, axis, base, block):
@@ -98,24 +99,24 @@
         self.copy(half, block(3, 1), axis, 3, base + 3)
 
     def first(self):
-        for half in range(2):
+        for half in self.halves:
             self.turn(half, 0, 0, lambda n, part=None: self.ref(half, n, 0, part))
-        for half in range(2):
+        for half in self.halves:
             self.both(half, 1)
             self.both(half, 3)
 
     def second(self):
-        for half in range(2):
+        for half in self.halves:
             for part in range(2):
                 self.wait(half, self.ref(half, 2, 0, part), 2 + part)
             self.both(half, 2)
 
     def third(self, j):
-        for half in range(2):
+        for half in self.halves:
             self.turn(half, 1, 4 + 4 * j, lambda n, part=None: self.ref(half, j, n, part))
 
     def fourth(self, j):
-        for half in range(2):
+        for half in self.halves:
             for part in range(2):
                 self.wait(half, self.ref(half, j, 2, part), 6 + 4 * j + part)
 
@@ -193,36 +194,36 @@
 
     def first(src, dst, to_y, send, recv):
         is_self = jnp.logical_and(to_y == y, h == core)
-        for dz in (0, 1, 7, 2, 6, 3, 5, 4):
-            c = remote(src, dst, send.at[dz], recv, dev(to_y, x, (z + dz) % 8, h))
-            if dz:
-                c.start()
-            else:
-
-                @pl.when(is_self)
-                def _():
-                    pltpu.make_async_copy(src, dst, recv).start()
-
-                @pl.when(jnp.logical_not(is_self))
-                def _():
-                    c.start()
+
+        def copy(dz):
+            return remote(src, dst, send.at[dz], recv, dev(to_y, x, (z + dz) % 8, h))
+
+        def start():
+            for dz in (1, 7, 2, 6, 3, 5, 4):
+                copy(dz).start()
+
+            @pl.when(is_self)
+            def _():
+                pltpu.make_async_copy(src, dst, recv).start()
+
+            @pl.when(jnp.logical_not(is_self))
+            def _():
+                copy(0).start()
 
         def done():
-            for dz in range(8):
-                if dz:
-                    wait_bytes(src, send.at[dz])
-                else:
-
-                    @pl.when(jnp.logical_not(is_self))
-                    def _():
-                        wait_bytes(src, send.at[0])
-
-        return done
-
-    dones = [
-        first(bst, bcs.at[zc, core], y, bsend, brecv.at[zc, core]),
-        first(zx, own_z(inner_side, ys, zl, core), y_to, zsend, zrecv.at[inner_side, zl, core]),
-    ]
+            for dz in range(1, 8):
+                wait_bytes(src, send.at[dz])
+
+            @pl.when(jnp.logical_not(is_self))
+            def _():
+                wait_bytes(src, send.at[0])
+
+        return start, done
+
+    bc_start, bc_done = first(bst, bcs.at[zc, core], y, bsend, brecv.at[zc, core])
+    zx_start, zx_done = first(zx, own_z(inner_side, ys, zl, core), y_to, zsend, zrecv.at[inner_side, zl, core])
+    bc_start()
+    zx_start()
     merge = remote(ow, ows.at[core], swap_s.at[2], swap_r.at[2], partner)
     merge.start()
     merge_own = pltpu.make_async_copy(ow, ows.at[core], local.at[2])
@@ -249,22 +250,21 @@
     far_lanes = pl.multiple_of(1024 * (1 - core), 1024)
 
     def view_o1(half, sy, sx, part):
-        lanes = pl.ds(my_lanes + 256 * half, 256) if part is None else pl.ds(my_lanes + 256 * half + 128 * part, 128)
+        size = 256 if half else PLANE_FIRST - 256
+        base = my_lanes + half * (PLANE_FIRST - 256)
+        lanes = pl.ds(base, size) if part is None else pl.ds(base + size // 2 * part, size // 2)
         return wo.at[sy, sx % 2, z, sx // 2, :, lanes]
 
     def view_o2(half, sy, sx, part):
-        zs = pl.ds(4 * half, 4) if part is None else pl.ds(4 * half + 2 * part, 2)
-        return wo.at[sy, sx % 2, zs, sx // 2, :, pl.ds(my_lanes + 512, 512)]
+        zs = pl.ds(0, 8) if part is None else pl.ds(4 * part, 4)
+        return wo.at[sy, sx % 2, zs, sx // 2, :, pl.ds(my_lanes + PLANE_FIRST, 1024 - PLANE_FIRST)]
 
     def plane(zsrc, part, base=None):
-        return wo.at[:, :, zsrc, :, :, pl.ds((my_lanes if base is None else base) + 256 * part, 256)]
-
-    def corner(half, j, base):
-        lanes = pl.ds(base + 512, 512)
-        if half == 0:
-            return wo.at[(y - j) % 4, :, pl.ds(0, 4), :, :, lanes]
+        return wo.at[:, :, zsrc, :, :, pl.ds((my_lanes if base is None else base) + PLANE_FIRST // 2 * part, PLANE_FIRST // 2)]
+
+    def corner(j, base):
         sx = (x - j) % 4
-        return wo.at[:, sx % 2, pl.ds(4, 4), sx // 2, :, lanes]
+        return wo.at[:, sx % 2, :, sx // 2, :, pl.ds(base + PLANE_FIRST, 1024 - PLANE_FIRST)]
 
     o_copies = []
 
@@ -303,7 +303,7 @@
     set_i = Ring(view_g(1), same, gs.at[1], gr.at[1])
     set_g = Ring(view_g(0), flip, gs.at[2], gr.at[2])
     set_o = Ring(view_o1, same, gs.at[3], gr.at[3])
-    set_p = Ring(view_o2, same, gs.at[4], gr.at[4])
+    set_p = Ring(view_o2, same, gs.at[4], gr.at[4], (1,))
 
     merge_own.wait()
     wait_bytes(ows.at[1 - core], swap_r.at[2])
@@ -364,10 +364,6 @@
 
 
     set_o.first()
-    set_o.second()
-    for j in (0, 1, 3, 2):
-        set_o.third(j)
-
     for q in range(4):
         for s in range(2):
             wait_bytes(bcs.at[q, s], brecv.at[q, s])
@@ -385,31 +381,36 @@
         for q in range(2):
             wait_bytes(own_z(1, y, s, q), zrecv.at[1, s, q])
     set_i.begin()
+    set_o.second()
+    set_b.first()
+    set_i.first()
+    for j in (0, 1, 3, 2):
+        set_o.third(j)
+    for k in (1, 7, 2, 6, 3, 5, 4):
+        ref = wo.at[y, xl, z, xh, :, pl.ds(my_lanes + PLANE_FIRST, 1024 - PLANE_FIRST)]
+        cp = remote(ref, ref, o2s.at[k - 1], o2r.at[k - 1], dev(y, x, (z + k) % 8, core))
+        cp.start()
+        o_copies.append(cp)
+    set_b.second()
+    set_i.second()
     for j in range(4):
         set_o.fourth(j)
     for part in range(2):
         for way in range(2):
             o_send(z, way, 0, part)
     o_swap(z, 0)
-    set_b.first()
-    set_i.first()
-    for k in (1, 7, 2, 6, 3, 5, 4):
-        ref = wo.at[y, xl, z, xh, :, pl.ds(my_lanes + 512, 512)]
-        cp = remote(ref, ref, o2s.at[k - 1], o2r.at[k - 1], dev(y, x, (z + k) % 8, core))
-        cp.start()
-        o_copies.append(cp)
-    set_b.second()
-    set_i.second()
     for j in (0, 1, 3, 2):
         set_b.third(j)
         set_i.third(j)
-        if j == 1:
-            o_turn(1)
     for j in range(4):
         set_b.fourth(j)
     swaps = [remote(wb.at[:, core], wb.at[:, core], swap_s.at[1], swap_r.at[1], partner)]
     swaps[0].start()
-    o_turn(2)
+    for s in range(2):
+        for q in range(2):
+            wait_bytes(own_z(0, flip(y), s, q), zrecv.at[0, s, q])
+    set_g.begin()
+    o_turn(1)
     wait_bytes(wb.at[:, 1 - core], swap_r.at[1])
     bco[...] = dot_nt(xs[...].reshape(ROWS, 2048), wb[...].reshape(512, 2048)).astype(BF16)
 
@@ -431,13 +432,6 @@
 
     for j in range(4):
         set_i.fourth(j)
-    for s in range(2):
-        for q in range(2):
-            wait_bytes(own_z(0, flip(y), s, q), zrecv.at[0, s, q])
-    set_g.begin()
-    for k in range(1, 8):
-        wait_bytes(wo.at[y, xl, (z - k) % 8, xh, :, pl.ds(my_lanes + 512, 512)], o2r.at[k - 1])
-    set_p.begin()
     for g in range(4):
         w = wz[1, g].reshape(256, 2048)
         inner[:, 256 * g : 256 * g + 256] = dot_nt(xs[...].reshape(ROWS, 2048), w).astype(BF16)
@@ -479,9 +473,14 @@
             if d == 0:
                 pay[j, 64:80, :] = tail[:, 128 * q : 128 * q + 128]
         state_copies += send_states(pay, (got_f, got_b)[d], s1.at[d], r1.at[d])
-    o_turn(3)
     set_g.first()
+    o_turn(2)
     set_g.second()
+    for k in range(1, 8):
+        lanes = pl.ds(my_lanes + PLANE_FIRST, 1024 - PLANE_FIRST)
+        wait_bytes(wo.at[y, xl, (z - k) % 8, xh, :, lanes], o2r.at[k - 1])
+    set_p.begin()
+    set_g.third(0)
 
     left = lax.broadcasted_iota(jnp.int32, (BLOCK, BLOCK), 1) < 64
 
@@ -508,19 +507,19 @@
             state = de * state + got[i, :64, :].astype(F32)
         state_copies += send_states(reply.at[d], ent.at[d], s2.at[d], r2.at[d])
         if d == 0:
-            set_p.first()
-            set_p.second()
-    for j in (0, 1, 3, 2):
-        set_g.third(j)
-    o_turn(4)
-    for j in (0, 1, 3, 2):
-        set_p.third(j)
+            for j in (1, 3, 2):
+                set_g.third(j)
+    set_p.first()
+    set_p.second()
+    o_turn(3)
     for j in range(4):
         set_g.fourth(j)
     for g in range(4):
         w = wz[0, g].reshape(256, 2048)
         gate = dot_nt(xs[...].reshape(ROWS, 2048), w).astype(BF16).astype(F32)
         wide_f[0, :, 256 * g : 256 * g + 256] = gate / (1.0 + jnp.exp(-gate))
+    for j in (0, 1, 3, 2):
+        set_p.third(j)
     for d in range(2):
         wait_states(ent.at[d], r2.at[d])
         for q in range(8):
@@ -556,10 +555,10 @@
     cp.start()
     pair_copies.append(cp)
 
+    o_turn(4)
     for j in (0, 1, 3, 2):
         set_p.fourth(j)
-        for half in range(2):
-            o_hand(corner(half, j, my_lanes), 16 + 2 * j + half)
+        o_hand(corner(j, my_lanes), 16 + j)
     for i in range(8):
         wait_bytes(wide.at[:, pl.ds(natural(1 - core, i), 128)], pr.at[i])
     wait_bytes(sqf, pr.at[8])
@@ -568,14 +567,13 @@
         for part in range(2):
             wait_bytes(plane((z - d) % 8, part, far_lanes), osw_r.at[2 * d + part])
     for j in range(4):
-        for half in range(2):
-            wait_bytes(corner(half, j, far_lanes), osw_r.at[16 + 2 * j + half])
+        wait_bytes(corner(j, far_lanes), osw_r.at[16 + j])
     for g in range(8):
         w = wo[g // 2, g % 2].reshape(256, 2048)
         result[:, 256 * g : 256 * g + 256] = (dot_nt(wide[...], w) * scale).astype(BF16)
 
-    for done in dones:
-        done()
+    bc_done()
+    zx_done()
     for s in (set_b, set_i, set_g, set_o, set_p):
         s.drain()
     tok_far.wait_send()

time: 124 us -> 115 us (0.927)
  Pallas kernels: 122 us -> 112 us
    pallas_call x1, Pallas kernels: 122 us -> 112 us  [layer(): pl.pallas_call(kernel, out_shape=jax.ShapeDtypeStruct((256, 2048), BF16),...]
where the time goes in v5:
time: 115 us; the launch traced here: 114 us
  Pallas kernels  112 us (97%)
  local copies, waits for them, and re-layouts  2.3 us (2%)
    pallas_call x1, Pallas kernels, layer(): pl.pallas_call(kernel, out_shape=jax.ShapeDtypeStruct((256, 2048), BF16),...  112 us
    unnamed x1, local copies, waits for them, and re-layouts  2.3 us

profile of v5, /device:TPU:1, one launch (start us, length us, event | category | flops | bytes accessed | tf_op | source)
XLA Modules:
  0.0 114.5 jit_solution(13096133208342170148)
XLA Ops:
  0.0 112.2 %layer.1 = bf16[256,2048]{1,0:T(8,128)(2,1)} custom-call(bf16[16,2048]{1,0:T(8,128)(2,1)} %bitcast.18, bf16[2,2048]{1,0:T(2,128)(2,1)} %bitcast.20, bf16[16,1024]{1,0:T(8,128)(2,1)} %bitcast.19, bf16[256,2048]{1,0:T(8,128)(2,1)} %bitcast.16, bf16[64,2048]{1,0:T(8,128)(2,1)} %bitcast.17, f32[1,32]{1,0:T(1,128)} %bitcast.22, f32[1,32]{1,0:T(1,128)} %bitcast.23, ...), custom_call_target="tpu_custom_call" | custom-call | tf_op jit(solution)/shard_map/layer/pallas_call | solution.py:592
  112.2 2.3 %copy.10 = bf16[1,256,2048]{2,1,0:T(8,128)(2,1)} copy(bf16[1,256,2048]{2,1,0:T(8,128)(2,1)} %bitcast.15) | data formatting | bytes 2097152
